TPU v7x, 32 devices: a whole 2x2x4 slice. The times are simulated.
32 devices in a mesh: dp: 2 (over y), ctx: 16 (over z, x, core).
Axes of the slice: x: 2, y: 2, z: 4, core: 2. Of those that a mesh axis runs over, the one named last changes fastest.
Arguments:
- base_ids: int32 [8192], P(('dp', 'ctx')), parts along dimension 0, may hold values from 0 to 4
- complement: int32 [5], replicated, may hold values from 0 to 4, each once
- embedding: bfloat16 [5, 768], replicated, may hold values from -6 to 6
- w_gate: bfloat16 [768, 768], replicated, may hold values from -0.21875 to 0.21875
- w_mix: bfloat16 [768, 1024], replicated, may hold values from -0.21875 to 0.21875
- w_step: bfloat16 [768, 12], replicated, may hold values from -0.21875 to 0.21875
- step_bias: float32 [12], replicated, may hold values from -3 to -1
- decay_rate: float32 [12], replicated, may hold values from 0.0001 to 0.5, as said below
- conv_weight: float32 [4, 1024], replicated, may hold values from -3 to 3
- conv_bias: float32 [1024], replicated, may hold values from -3 to 3
- skip_gain: float32 [12], replicated, may hold values from 0.5 to 1.5
- norm_gain: float32 [768], replicated, may hold values from 0.5 to 1.5
- w_out: bfloat16 [768, 768], replicated, may hold values from -0.21875 to 0.21875
Outputs:
- mixed_out: bfloat16 [8192, 768], P(('dp', 'ctx')), parts along dimension 0
There are 2 independent parts, one for each index of `dp`. A program takes and returns all parts, laid end to end along the dimension named above; an argument that names none is the same for every part. Nothing has to cross between parts.
Inputs may be any that keep to these rules, and one draw needn't show every extreme that they name: `base_ids`: base codes. `complement`: each code appears once. `decay_rate`: positive per-head rates.
All inputs are finite; a program needn't handle non-finite values.
Results may differ from a plain program's by a relative error of at most 0.0062.
Values may be sent and summed in bfloat16 or wider, within the bound.
No kernel may reach another device: no remote copies, remote signals or barrier semaphores. Data moves between devices by JAX's collectives and lax.ppermute only.
A program may use at most 256 MiB of HBM per device.

v0:
```python
import jax
import jax.numpy as jnp
from jax import lax
from jax.sharding import PartitionSpec as P

exact_mode = lax.Precision.HIGHEST


def swapped(block, axis, stride):
    count = lax.axis_size(axis)
    route = []
    for low in range(count):
        high = low | 1 << stride
        if high != low and high < count:
            route += [(low, high), (high, low)]
    return lax.ppermute(block, axis, route)


def padded(value, sides, width):
    for axis, dim in sides:
        size, length = (lax.axis_size(axis), value.shape[dim])
        up = [(i, (i + 1) % size) for i in range(size - 1)]
        down = [(j, i) for i, j in up]
        last = lax.slice_in_dim(value, length - width, length, axis=dim)
        leading = lax.slice_in_dim(value, 0, width, axis=dim)
        before = lax.ppermute(last, axis, up)
        after = lax.ppermute(leading, axis, down)
        value = jnp.concatenate([before, value, after], axis=dim)
    return value


def entering(value, axis, combine, identity, reverse):
    size, position = (lax.axis_size(axis), lax.axis_index(axis))
    everything = jax.tree.map(lambda part: lax.all_gather(part, axis), value)
    start = jax.tree.map(
        lambda part, zero: jnp.broadcast_to(jnp.asarray(zero, part.dtype), part.shape),
        value,
        identity,
    )

    def turn(k, before):
        at = size - 1 - k if reverse else k
        reached = at > position if reverse else at < position
        new = combine(before, jax.tree.map(lambda part: part[at], everything))
        return jax.tree.map(lambda a, b: jnp.where(reached, a, b), new, before)

    return lax.fori_loop(0, size, turn, start)


def lookup_rows(ident_rows, lookup_table):
    table_rows = lookup_table.shape[0]
    onehot = (ident_rows[..., None] == jnp.arange(table_rows, dtype=jnp.int32)).astype(
        lookup_table.dtype
    )
    return jnp.einsum(
        "...v,vc->...c",
        onehot,
        lookup_table,
        preferred_element_type=jnp.float32,
        precision=exact_mode,
    )


def block_pass(carry_pair, inputs):
    carried_state, offset = carry_pair
    values, keys_b, reads_c, log_decay, step_sizes = inputs
    cumulative = jnp.cumsum(log_decay, axis=0)
    headwise = jnp.transpose(cumulative)
    gaps_log = headwise[:, :, None] - headwise[:, None, :]
    block_size = cumulative.shape[0]
    causal = (jnp.arange(block_size)[:, None] >= jnp.arange(block_size)[None, :])[None]
    decays = jnp.where(causal, jnp.exp(jnp.where(causal, gaps_log, 0.0)), 0.0)
    scores = jnp.dot(reads_c, keys_b.T, precision=exact_mode)
    weights = scores[None] * decays * jnp.transpose(step_sizes)[:, None, :]
    inner_out = jnp.einsum("hts,shp->thp", weights, values, precision=exact_mode)
    carried = jnp.exp(cumulative)[:, :, None] * jnp.einsum(
        "tn,hpn->thp", reads_c, carried_state, precision=exact_mode
    )
    tail_weight = jnp.exp(cumulative[-1][None, :] - cumulative) * step_sizes
    weighted_values = tail_weight[:, :, None] * values
    carried_state = jnp.exp(cumulative[-1])[:, None, None] * carried_state + jnp.einsum(
        "shp,sn->hpn", weighted_values, keys_b, precision=exact_mode
    )
    return (
        (carried_state, offset + cumulative[-1]),
        (inner_out + carried, offset[None, :] + cumulative),
    )


def local_pass(
    rows_ext,
    raw_steps,
    conv_weight,
    conv_bias,
    step_bias,
    decay_rate,
    head_count,
    head_dim,
    state_dim,
):
    length = raw_steps.shape[0]
    tap_count = conv_weight.shape[0]
    widened = rows_ext.astype(jnp.float32)
    summed = conv_bias[None, :] + sum(
        (
            conv_weight[tap_index][None, :] * widened[tap_index : tap_index + length]
            for tap_index in range(tap_count)
        )
    )
    conv_out = jax.nn.silu(summed)
    inner_dim = head_count * head_dim
    values = conv_out[:, :inner_dim].reshape(length, head_count, head_dim)
    keys_b = conv_out[:, inner_dim : inner_dim + state_dim]
    reads_c = conv_out[:, inner_dim + state_dim :]
    step_sizes = jax.nn.softplus(raw_steps + step_bias[None, :])
    log_decay = -step_sizes * decay_rate[None, :]
    block_rows = min(256, length)
    block_count = length // block_rows
    shaped = (
        values.reshape(block_count, block_rows, head_count, head_dim),
        keys_b.reshape(block_count, block_rows, state_dim),
        reads_c.reshape(block_count, block_rows, state_dim),
        log_decay.reshape(block_count, block_rows, head_count),
        step_sizes.reshape(block_count, block_rows, head_count),
    )
    initial = (
        jnp.zeros((head_count, head_dim, state_dim), jnp.float32),
        jnp.zeros((head_count,), jnp.float32),
    )
    finals, outputs = lax.scan(block_pass, initial, shaped)
    partial_value = outputs[0].reshape(length, head_count, head_dim)
    cumulative = outputs[1].reshape(length, head_count)
    return (finals[0], jnp.exp(finals[1]), partial_value, cumulative, values, reads_c)


def finish(local_parts, incoming_state, gate_rows, skip_gain, norm_gain):
    final_state, growth, partial_value, cumulative, values, reads_c = local_parts
    ssm_out = (
        partial_value
        + jnp.exp(cumulative)[:, :, None]
        * jnp.einsum("tn,hpn->thp", reads_c, incoming_state, precision=exact_mode)
        + skip_gain[None, :, None] * values
    )
    length = ssm_out.shape[0]
    gated = ssm_out.reshape(length, -1) * jax.nn.silu(gate_rows)
    inverse_rms = lax.rsqrt(jnp.mean(gated * gated, axis=1, keepdims=True) + 1e-05)
    return gated * inverse_rms * norm_gain[None, :]


def combine(first_part, second_part):
    return (
        first_part[0] * second_part[0],
        first_part[1] * second_part[0][:, None, None] + second_part[1],
        first_part[2] * second_part[2],
        first_part[3] * second_part[2][:, None, None] + second_part[3],
    )


def on_device(
    base_ids,
    complement,
    embedding,
    w_gate,
    w_mix,
    w_step,
    step_bias,
    decay_rate,
    conv_weight,
    conv_bias,
    skip_gain,
    norm_gain,
    w_out,
):
    length = base_ids.shape[0]
    letter_count = embedding.shape[0]
    head_count = decay_rate.shape[0]
    inner_dim = w_gate.shape[1]
    head_dim = inner_dim // head_count
    state_dim = (w_mix.shape[1] - inner_dim) // 2
    rim_width = conv_weight.shape[0] - 1
    members = lax.axis_size("ctx")
    position = lax.axis_index("ctx")
    gate_table = jnp.dot(embedding, w_gate, preferred_element_type=jnp.float32).astype(jnp.bfloat16)
    mix_table = jnp.dot(embedding, w_mix, preferred_element_type=jnp.float32).astype(jnp.bfloat16)
    step_table = jnp.dot(embedding, w_step, preferred_element_type=jnp.float32)
    letters = jnp.arange(letter_count, dtype=jnp.int32)
    mirrored = base_ids
    for bit_index in range(members.bit_length() - 1):
        mirrored = swapped(mirrored, "ctx", bit_index)
    second = jnp.sum(
        jnp.where(mirrored[::-1][:, None] == letters[None, :], complement[None, :], 0), axis=1
    )
    strand_ids = jnp.stack([base_ids, second])
    mixed = lookup_rows(strand_ids, mix_table).astype(jnp.bfloat16)
    extended = padded(mixed, (("ctx", 1),), rim_width)
    slot_index = jnp.arange(length + 2 * rim_width)
    valid_rows = jnp.logical_and(
        jnp.logical_or(slot_index >= rim_width, position > 0),
        jnp.logical_or(slot_index < length + rim_width, position < members - 1),
    )
    extended = jnp.where(valid_rows[None, :, None], extended, jnp.zeros_like(extended))
    gate_rows = lookup_rows(strand_ids, gate_table)
    raw_steps = lookup_rows(strand_ids, step_table)
    forward_runs = [
        local_pass(
            extended[strand, : length + rim_width],
            raw_steps[strand],
            conv_weight,
            conv_bias,
            step_bias,
            decay_rate,
            head_count,
            head_dim,
            state_dim,
        )
        for strand in range(2)
    ]
    backward_runs = [
        local_pass(
            extended[strand, rim_width:][::-1],
            raw_steps[strand][::-1],
            conv_weight,
            conv_bias,
            step_bias,
            decay_rate,
            head_count,
            head_dim,
            state_dim,
        )
        for strand in range(2)
    ]
    unit_decay = jnp.ones((head_count,), jnp.float32)
    empty_state = jnp.zeros((head_count, head_dim, state_dim), jnp.float32)
    identity = (unit_decay, empty_state, unit_decay, empty_state)
    into_ahead = entering(
        (forward_runs[0][1], forward_runs[0][0], forward_runs[1][1], forward_runs[1][0]),
        "ctx",
        combine,
        identity,
        False,
    )
    into_behind = entering(
        (backward_runs[0][1], backward_runs[0][0], backward_runs[1][1], backward_runs[1][0]),
        "ctx",
        combine,
        identity,
        True,
    )
    strand_sums = []
    for strand in range(2):
        forward = finish(
            forward_runs[strand],
            into_ahead[2 * strand + 1],
            gate_rows[strand],
            skip_gain,
            norm_gain,
        )
        backward = finish(
            backward_runs[strand],
            into_behind[2 * strand + 1],
            gate_rows[strand][::-1],
            skip_gain,
            norm_gain,
        )[::-1]
        strand_sums.append((forward + backward).astype(jnp.bfloat16))
    second_sum = strand_sums[1]
    for bit_index in range(members.bit_length() - 1):
        second_sum = swapped(second_sum, "ctx", bit_index)
    second_sum = second_sum[::-1]
    result = jnp.dot(strand_sums[0], w_out, preferred_element_type=jnp.float32) + jnp.dot(
        second_sum, w_out, preferred_element_type=jnp.float32
    )
    return result.astype(jnp.bfloat16)


def solution(mesh):
    return jax.shard_map(
        on_device,
        mesh=mesh,
        in_specs=(P(("dp", "ctx")), P(), P(), P(), P(), P(), P(), P(), P(), P(), P(), P(), P()),
        out_specs=P(("dp", "ctx"), None),
        check_vma=False,
    )
```

profile of v0, /device:TPU:0, one launch (start us, length us, event | category | flops | bytes accessed | tf_op | source)
XLA Modules:
  0.0 412.7 jit_solution(11430521690861173924)
XLA Ops:
  36.3 11.8 %rev.31 = bf16[259,1024]{1,0:T(8,128)(2,1)} reverse(bf16[259,1024]{1,0:T(8,128)(2,1)} %get-tuple-element.572), dimensions={0} | reverse | bytes 1060864 | tf_op jit(solution)/shard_map/rev | solution.py:220
  49.2 11.7 %rev.34 = bf16[259,1024]{1,0:T(8,128)(2,1)} reverse(bf16[259,1024]{1,0:T(8,128)(2,1)} %get-tuple-element.571), dimensions={0} | reverse | bytes 1060864 | tf_op jit(solution)/shard_map/rev | solution.py:220
  95.8 6.9 %rev.37 = f32[256,768]{1,0:T(8,128)} reverse(f32[256,768]{1,0:T(8,128)} %get-tuple-element.568), dimensions={0} | reverse | bytes 1572864 | tf_op jit(solution)/shard_map/rev | solution.py:261
  105.0 6.8 %rev.35 = f32[256,768]{1,0:T(8,128)} reverse(f32[256,768]{1,0:T(8,128)} %get-tuple-element.567), dimensions={0} | reverse | bytes 1572864 | tf_op jit(solution)/shard_map/rev | solution.py:261
  111.9 22.0 %all-gather.6 = f32[16,1,12]{2,1,0:T(1,128)S(1)} all-gather(f32[1,1,12]{2,1,0:T(1,128)S(1)} %bitcast.341), channel_id=1, replica_groups=mesh['dp'=2,'ctx'=16] {'ctx'}, dimensions={0}, use_global_device_ids=true | all-gather | bytes 816 | tf_op jit(solution)/shard_map/all_gather | solution.py:34
  133.9 17.3 %all-gather.7 = f32[16,1,12]{2,1,0:T(1,128)S(1)} all-gather(f32[1,1,12]{2,1,0:T(1,128)S(1)} %bitcast.340), channel_id=1, replica_groups=mesh['dp'=2,'ctx'=16] {'ctx'}, dimensions={0}, use_global_device_ids=true | all-gather | bytes 816 | tf_op jit(solution)/shard_map/all_gather | solution.py:34
  151.2 18.7 %all-gather.4 = f32[16,1,12]{2,1,0:T(1,128)S(1)} all-gather(f32[1,1,12]{2,1,0:T(1,128)S(1)} %bitcast.339), channel_id=1, replica_groups=mesh['dp'=2,'ctx'=16] {'ctx'}, dimensions={0}, use_global_device_ids=true | all-gather | bytes 816 | tf_op jit(solution)/shard_map/all_gather | solution.py:34
  169.9 17.7 %all-gather.5 = f32[16,1,12]{2,1,0:T(1,128)S(1)} all-gather(f32[1,1,12]{2,1,0:T(1,128)S(1)} %bitcast.338), channel_id=1, replica_groups=mesh['dp'=2,'ctx'=16] {'ctx'}, dimensions={0}, use_global_device_ids=true | all-gather | bytes 816 | tf_op jit(solution)/shard_map/all_gather | solution.py:34
  191.7 5.0 %fusion.69 = f32[256,12,64]{0,2,1:T(8,128)S(1)} fusion(f32[256,12,64]{0,2,1:T(8,128)} %bitcast.291, f32[12,256]{1,0:T(8,128)S(1)} %copy-done.20, f32[12,256]{1,0:T(8,128)S(1)} %bitcast.317, f32[256,256]{1,0:T(8,128)S(1)} %fusion.136, pred[256,256]{1,0:T(8,128)(4,1)S(1)} %copy-done.15), kind=kOutput, calls=%fused_computation.72 | convolution fusion | flops 607911936 | bytes 1925120 | tf_op jit(solution)/shard_map/while/body/eval_jaxpr/hts,shp->thp/dot_general | solution.py:75
  199.3 3.7 fusion.66
  205.7 3.7 fusion.63
  212.0 21.7 %while.23 = (s32[]{:T(128)}, f32[12,64,128]{2,1,0:T(8,128)S(1)}, f32[12,64,128]{2,1,0:T(8,128)S(1)}, s32[]{:T(128)}, f32[16,12]{1,0:T(8,128)S(1)}, /*index=5*/f3...) while((s32[]{:T(128)}, f32[12,64,128]{2,1,0:T(8,128)S(1)}, ...), condition=%wide.region_13.14_spmd.clone, body=%wide.region_12.13_spmd.clone.sunk | while | flops 786440 | bytes 2359787 | solution.py:47
  233.7 3.1 fusion.73
  243.4 6.8 %rev.38 = f32[256,768]{1,0:T(8,128)} reverse(f32[256,768]{1,0:T(8,128)} %multiply_multiply_fusion), dimensions={0} | reverse | bytes 1572864 | tf_op jit(solution)/shard_map/rev | solution.py:258
  250.3 10.1 %all-gather.13.cloned.1.call-done = f32[192,64,128]{2,1,0:T(8,128)} async-done(((f32[12,64,128]{2,1,0:T(8,128)}), f32[192,64,128]{2,1,0:T(8,128)}) %all-gather.13.cloned.1.call-update) | async-done | bytes 6291472 | tf_op jit(solution)/shard_map/all_gather | solution.py:34
  260.4 62.6 %all-gather.15.cloned.1.call-done = f32[192,64,128]{2,1,0:T(8,128)} async-done(((f32[12,64,128]{2,1,0:T(8,128)}), f32[192,64,128]{2,1,0:T(8,128)}) %all-gather.15.cloned.1.call-update) | async-done | bytes 6291472 | tf_op jit(solution)/shard_map/all_gather | solution.py:34
  323.0 21.7 %while.22 = (s32[]{:T(128)}, f32[12,64,128]{2,1,0:T(8,128)S(1)}, f32[12,64,128]{2,1,0:T(8,128)S(1)}, s32[]{:T(128)}, f32[16,12]{1,0:T(8,128)S(1)}, /*index=5*/f3...) while((s32[]{:T(128)}, f32[12,64,128]{2,1,0:T(8,128)S(1)}, ...), condition=%wide.region_6.7_spmd.clone, body=%wide.region_5.6_spmd.clone.sunk | while | flops 786436 | bytes 2359725 | solution.py:47
  344.7 3.5 multiply_reduce_fusion.1
  364.0 5.1 %fusion.60 = f32[256,12,64]{0,2,1:T(8,128)S(1)} fusion(f32[256,12,64]{0,2,1:T(8,128)} %bitcast.294, f32[12,256]{1,0:T(8,128)S(1)} %copy-done.17, f32[12,256]{1,0:T(8,128)S(1)} %bitcast.311, f32[256,256]{1,0:T(8,128)S(1)} %fusion.146, pred[256,256]{1,0:T(8,128)(4,1)S(1)} %copy-done.15), kind=kOutput, calls=%fused_computation.69 | convolution fusion | flops 607911936 | bytes 1925120 | tf_op jit(solution)/shard_map/while/body/eval_jaxpr/hts,shp->thp/dot_general | solution.py:75
  369.1 4.2 %collective-permute-done.7 = bf16[256,768]{1,0:T(8,128)(2,1)S(1)} collective-permute-done((bf16[256,768]{1,0:T(8,128)(2,1)S(1)}, bf16[256,768]{1,0:T(8,128)(2,1)S(1)}, u32[]{:S(2)}, u32[]{:S(2)}) %collective-permute-start.7) | collective-permute-done | bytes 393248 | tf_op jit(solution)/shard_map/ppermute | solution.py:16
  379.5 4.5 %collective-permute-done.8 = bf16[256,768]{1,0:T(8,128)(2,1)} collective-permute-done((bf16[256,768]{1,0:T(8,128)(2,1)S(1)}, bf16[256,768]{1,0:T(8,128)(2,1)}, u32[]{:S(2)}, u32[]{:S(2)}) %collective-permute-start.8) | collective-permute-done | bytes 393248 | tf_op jit(solution)/shard_map/ppermute | solution.py:16
  385.9 3.9 rev.36
  392.1 3.5 fusion.119
  395.6 7.5 %collective-permute-done.9 = bf16[256,768]{1,0:T(8,128)(2,1)S(1)} collective-permute-done((bf16[256,768]{1,0:T(8,128)(2,1)}, bf16[256,768]{1,0:T(8,128)(2,1)S(1)}, u32[]{:S(2)}, u32[]{:S(2)}) %collective-permute-start.9) | collective-permute-done | bytes 393248 | tf_op jit(solution)/shard_map/ppermute | solution.py:16
  (296 shorter events, 157.0 us)
Async XLA Ops:
  6.5 27.1 %copy-start.23 = (f32[12]{0:T(128)S(1)}, f32[12]{0:T(128)}, u32[]{:S(2)}) copy-start(f32[12]{0:T(128)} %param.23) | copy-start | bytes 148
  6.5 205.5 %all-gather.17.cloned.1.call-start = ((), (), s32[]{:S(2)}) async-start(), calls=%async_computation.2 | async-start | bytes 6684672 | tf_op jit(solution)/shard_map/all_gather | solution.py:34
  6.5 1.5 collective-permute-start
  8.0 4.4 %collective-permute-start.1 = (s32[256]{0:T(256)S(1)}, s32[256]{0:T(256)S(1)}, u32[]{:S(2)}, u32[]{:S(2)}) collective-permute-start(s32[256]{0:T(256)S(1)} %collective-permute-done), channel_id=1, source_target_pairs={{0,2},{2,0},{1,3},{3,1},{4,6},{6,4},{5,7},{7,5},{8,10},{10,8},{9,1... | collective-permute-start | bytes 3080 | tf_op jit(solution)/shard_map/ppermute | solution.py:16
  12.4 3.7 collective-permute-start.2
  16.0 4.6 %collective-permute-start.3 = (s32[256]{0:T(256)S(1)}, s32[256]{0:T(256)S(1)}, u32[]{:S(2)}, u32[]{:S(2)}) collective-permute-start(s32[256]{0:T(256)S(1)} %collective-permute-done.2), channel_id=1, source_target_pairs={{0,8},{8,0},{1,9},{9,1},{2,10},{10,2},{3,11},{11,3},{4,12},{12,4},... | collective-permute-start | bytes 3080 | tf_op jit(solution)/shard_map/ppermute | solution.py:16
  22.7 11.7 %collective-permute-start.5 = (bf16[2,3,1024]{2,1,0:T(4,128)(2,1)S(1)}, bf16[2,3,1024]{2,1,0:T(4,128)(2,1)S(1)}, u32[]{:S(2)}, u32[]{:S(2)}) collective-permute-start(bf16[2,3,1024]{2,1,0:T(4,128)(2,1)S(1)} %get-tuple-element.575), channel_id=1, source_target_pairs={{1,0},{2,1},{3,2},{4,3},{5,4},{6,5},{7,6},{8,7},{9,8},{10,9},{11,1... | collective-permute-start | bytes 36872 | tf_op jit(solution)/shard_map/ppermute | solution.py:27
  24.0 10.4 %collective-permute-start.4 = (bf16[2,3,1024]{2,1,0:T(4,128)(2,1)S(1)}, bf16[2,3,1024]{2,1,0:T(4,128)(2,1)S(1)}, u32[]{:S(2)}, u32[]{:S(2)}) collective-permute-start(bf16[2,3,1024]{2,1,0:T(4,128)(2,1)S(1)} %get-tuple-element.574), channel_id=1, source_target_pairs={{0,1},{1,2},{2,3},{3,4},{4,5},{5,6},{6,7},{7,8},{8,9},{9,10},{10,1... | collective-permute-start | bytes 36872 | tf_op jit(solution)/shard_map/ppermute | solution.py:26
  36.3 25.9 %copy-start.21 = (f32[1024]{0:T(1024)S(1)}, f32[1024]{0:T(1024)}, u32[]{:S(2)}) copy-start(f32[1024]{0:T(1024)} %param.26) | copy-start | bytes 12292
  68.5 15.0 %copy-start.2 = (f32[256,768]{0,1:T(8,128)}, f32[256,768]{0,1:T(8,128)S(1)}, u32[]{:S(2)}) copy-start(f32[256,768]{0,1:T(8,128)S(1)} %copy.84) | copy-start | bytes 2359300
  71.1 141.0 %all-gather.19.cloned.1.call-start = ((), (), s32[]{:S(2)}) async-start(), calls=%async_computation.3 | async-start | bytes 6684672 | tf_op jit(solution)/shard_map/all_gather | solution.py:34
  76.1 184.3 %all-gather.13.cloned.1.call-start = ((), (), s32[]{:S(2)}) async-start(), calls=%async_computation | async-start | bytes 6684672 | tf_op jit(solution)/shard_map/all_gather | solution.py:34
  83.5 239.6 %all-gather.15.cloned.1.call-start = ((), (), s32[]{:S(2)}) async-start(), calls=%async_computation.1 | async-start | bytes 6684672 | tf_op jit(solution)/shard_map/all_gather | solution.py:34
  95.8 16.1 %copy-start.29 = (f32[12]{0:T(128)S(1)}, f32[12]{0:T(128)}, u32[]{:S(2)}) copy-start(f32[12]{0:T(128)} %get-tuple-element.613) | copy-start | bytes 148
  95.8 38.1 %copy-start.28 = (f32[12]{0:T(128)S(1)}, f32[12]{0:T(128)}, u32[]{:S(2)}) copy-start(f32[12]{0:T(128)} %get-tuple-element.527) | copy-start | bytes 148
  95.8 55.4 %copy-start.27 = (f32[12]{0:T(128)S(1)}, f32[12]{0:T(128)}, u32[]{:S(2)}) copy-start(f32[12]{0:T(128)} %get-tuple-element.615) | copy-start | bytes 148
  95.8 74.1 %copy-start.26 = (f32[12]{0:T(128)S(1)}, f32[12]{0:T(128)}, u32[]{:S(2)}) copy-start(f32[12]{0:T(128)} %get-tuple-element.523) | copy-start | bytes 148
  95.8 95.8 %copy-start.15 = (pred[256,256]{1,0:T(8,128)(4,1)S(1)}, pred[256,256]{1,0:T(8,128)(4,1)}, u32[]{:S(2)}) copy-start(pred[256,256]{1,0:T(8,128)(4,1)} %iota_compare_fusion) | copy-start | bytes 196612
  95.8 95.8 %copy-start.20 = (f32[12,256]{1,0:T(8,128)S(1)}, f32[12,256]{1,0:T(8,128)}, u32[]{:S(2)}) copy-start(f32[12,256]{1,0:T(8,128)} %get-tuple-element.605) | copy-start | bytes 36868
  212.0 21.7 %copy-start.24 = (f32[12]{0:T(128)S(1)}, f32[12]{0:T(128)}, u32[]{:S(2)}) copy-start(f32[12]{0:T(128)} %param.27) | copy-start | bytes 148
  359.6 2.6 collective-permute-start.6
  362.1 11.3 %collective-permute-start.7 = (bf16[256,768]{1,0:T(8,128)(2,1)S(1)}, bf16[256,768]{1,0:T(8,128)(2,1)S(1)}, u32[]{:S(2)}, u32[]{:S(2)}) collective-permute-start(bf16[256,768]{1,0:T(8,128)(2,1)S(1)} %collective-permute-done.6), channel_id=1, source_target_pairs={{0,2},{2,0},{1,3},{3,1},{4,6},{6,4},{5,7},{7,5},{8,10},{10,8},{9,1... | collective-permute-start | bytes 1179656 | tf_op jit(solution)/shard_map/ppermute | solution.py:16
  373.4 10.6 %collective-permute-start.8 = (bf16[256,768]{1,0:T(8,128)(2,1)S(1)}, bf16[256,768]{1,0:T(8,128)(2,1)}, u32[]{:S(2)}, u32[]{:S(2)}) collective-permute-start(bf16[256,768]{1,0:T(8,128)(2,1)S(1)} %collective-permute-done.7), channel_id=1, source_target_pairs={{0,4},{4,0},{1,5},{5,1},{2,6},{6,2},{3,7},{7,3},{8,12},{12,8},{9,1... | collective-permute-start | bytes 1179656 | tf_op jit(solution)/shard_map/ppermute | solution.py:16
  383.9 19.1 %collective-permute-start.9 = (bf16[256,768]{1,0:T(8,128)(2,1)}, bf16[256,768]{1,0:T(8,128)(2,1)S(1)}, u32[]{:S(2)}, u32[]{:S(2)}) collective-permute-start(bf16[256,768]{1,0:T(8,128)(2,1)} %collective-permute-done.8), channel_id=1, source_target_pairs={{0,8},{8,0},{1,9},{9,1},{2,10},{10,2},{3,11},{11,3},{4,12},{12,4},... | collective-permute-start | bytes 1179656 | tf_op jit(solution)/shard_map/ppermute | solution.py:16
  (20 other events, 153.5 us)
Sparse Core Ops, SparseCore 0:
  71.2 63.4 all-gather.16
  137.0 60.5 all-gather.18
  199.9 60.4 all-gather.12
  262.5 60.4 all-gather.14
where the time goes:
time: 418 us; the launch traced here: 413 us
  waiting for transfers between devices  91.9 us (22%)
  local copies, waits for them, and re-layouts  79.9 us (19%)
  blocking collectives  75.7 us (18%)
  matrix products  67 us (16%)
  other arithmetic  65.8 us (16%)
  starting transfers between devices  17.1 us (4%)
  between operations  13.8 us (3%)
    all_gather x4, blocking collectives, entering(): everything = jax.tree.map(lambda part: lax.all_gather(part, axis), value)  75.7 us
    all_gather x4, waiting for transfers between devices, entering(): everything = jax.tree.map(lambda part: lax.all_gather(part, axis), value)  72.7 us
    select_n x32, other arithmetic, turn(): return jax.tree.map(lambda a, b: jnp.where(reached, a, b), new, before)  41.1 us
    rev x2, local copies, waits for them, and re-layouts, on_device(): extended[strand, rim_width:][::-1]  23.6 us
    ppermute x8, waiting for transfers between devices, swapped(): return lax.ppermute(block, axis, route)  19.1 us
    dot_general x4, matrix products, block_pass(): jnp.einsum('hts,shp->thp', weights, values, precision=exact_mode)  17.6 us
    rev x2, local copies, waits for them, and re-layouts, on_device(): gate_rows[strand][::-1]  13.7 us
    ppermute x8, starting transfers between devices, swapped(): return lax.ppermute(block, axis, route)  12.6 us
  transfers between devices with their start and end apart: 14, of which 9 were waited for; matrix products, arithmetic and copies ran while one was open for 32% of the time, Pallas kernels for 0%

commit v1 on v0

v1 whole, which is shorter than its diff:
```python
import functools

import jax
import jax.numpy as jnp
from jax import lax
from jax.experimental import pallas as pl
from jax.experimental.pallas import tpu as pltpu
from jax.sharding import PartitionSpec as P

F32, BF16, I32 = jnp.float32, jnp.bfloat16, jnp.int32
LETTER_ROWS = 8
CHUNK = 128
VMEM = pltpu.VMEM


def dot(a, b, contract=((1,), (0,))):
    return lax.dot_general(a, b, (contract, ((), ())), preferred_element_type=F32)


TN = ((0,), (0,))
NT = ((1,), (1,))


def silu(x):
    half = 0.5 * x
    return half + half * jnp.tanh(half)


def split(x):
    high = x.astype(BF16).astype(F32)
    return high, x - high


def iota(shape, dim):
    return lax.broadcasted_iota(I32, shape, dim)


def onehot_rows(row):
    return jnp.where(jnp.broadcast_to(row, (LETTER_ROWS, row.shape[1])) == iota((LETTER_ROWS, row.shape[1]), 0), 1.0, 0.0)


def code_onehot(shape, code_dim):
    code, slot = iota(shape, code_dim), iota(shape, 1 - code_dim) & 31
    before, last = code & 127, code >> 7
    first = (before * 41) >> 10
    pair = (before * 205) >> 10
    second, third = pair - 5 * first, before - 5 * pair
    tap = slot >> 3
    digit = jnp.where(tap == 0, first, jnp.where(tap == 1, second, jnp.where(tap == 2, third, last)))
    return jnp.where(digit == (slot & 7), 1.0, 0.0).astype(BF16)


def head_spread(rows, columns, head_dim):
    low = iota((rows, columns), 0) * head_dim
    lane = iota((rows, columns), 1)
    return jnp.where((lane >= low) & (lane < low + head_dim), 1.0, 0.0)


def tables_kernel(
    comp, emb, w_gate, w_mix, w_step, step_bias, rate, conv_w, conv_b, skip,
    taps, taps_t, look, ldt, stept, stepk, skipx, xt, bt,
    e16, *, heads, head_dim, state,
):
    letters, inner = emb.shape[0], heads * head_dim
    e16[...] = jnp.zeros_like(e16)
    e16[0:letters, :] = emb[...].astype(F32)
    for v in range(letters):
        e16[LETTER_ROWS + v : LETTER_ROWS + v + 1, :] = e16[pl.ds(comp[v], 1), :]
    rows = e16[...].astype(BF16)
    mix = dot(rows, w_mix[...]).astype(BF16).astype(F32)
    gate = silu(dot(rows, w_gate[...]).astype(BF16).astype(F32))
    raw = dot(rows, w_step[...]) + step_bias[...]
    step = jnp.maximum(raw, 0.0) + jnp.log1p(jnp.exp(-jnp.abs(raw)))
    decay_t = jnp.transpose(-step * rate[...])
    step_t = jnp.transpose(step)
    for strand in range(2):
        at = slice(strand * LETTER_ROWS, (strand + 1) * LETTER_ROWS)
        ldt[strand * heads : (strand + 1) * heads, :] = decay_t[:, at]
        stept[strand * heads : (strand + 1) * heads, :] = step_t[:, at]
        for v in range(letters):
            stepk[strand * heads : (strand + 1) * heads, v * 128 : (v + 1) * 128] = jnp.broadcast_to(
                step_t[:, strand * LETTER_ROWS + v : strand * LETTER_ROWS + v + 1], (heads, 128)
            )
    spread = head_spread(heads, inner, head_dim).astype(BF16)
    for part, high_low in enumerate(split(step)):
        wide = dot(high_low.astype(BF16), spread)
        for strand in range(2):
            at = slice(strand * LETTER_ROWS, (strand + 1) * LETTER_ROWS)
            look[part * LETTER_ROWS : (part + 1) * LETTER_ROWS, (2 + strand) * inner : (3 + strand) * inner] = wide[at]
    for part, high_low in enumerate(split(gate)):
        for strand in range(2):
            at = slice(strand * LETTER_ROWS, (strand + 1) * LETTER_ROWS)
            look[part * LETTER_ROWS : (part + 1) * LETTER_ROWS, strand * inner : (strand + 1) * inner] = high_low[at]
    skip_high, skip_rest = split(skip[...])
    skip_mid, skip_low = split(skip_rest)
    skipx[...] = sum(dot(part.astype(BF16), spread) for part in (skip_high, skip_mid, skip_low))
    width = conv_w.shape[1]
    codes = xt.shape[2]
    by_column = code_onehot((64, codes), 1)
    by_row = code_onehot((codes, 64), 0)
    for strand in range(2):
        letter_rows = mix[strand * LETTER_ROWS : (strand + 1) * LETTER_ROWS]
        weighted = [conv_w[k : k + 1, :] * letter_rows for k in range(4)]
        weighted[3] = weighted[3] + conv_b[...]
        high, low = split(jnp.concatenate(weighted, axis=0))
        both = jnp.concatenate([high, low], axis=0)
        taps[:, strand * width : (strand + 1) * width] = both.astype(BF16)
        turned = jnp.transpose(both[:, :inner]).astype(BF16)
        taps_t[strand] = turned
        for low_row in range(0, inner, CHUNK):
            xt[strand, low_row : low_row + CHUNK, :] = silu(dot(turned[low_row : low_row + CHUNK], by_column)).astype(BF16)
        bt[strand] = silu(dot(by_row, both[:, inner : inner + state].astype(BF16))).astype(BF16)


def local_kernel(
    near, taps, look, ldt, skipx,
    yg, eg, reads,
    *, heads, head_dim, state,
):
    length, inner = near.shape[1], heads * head_dim
    width = inner + 2 * state
    blocks = length // CHUNK
    ahead = jnp.concatenate([onehot_rows(near[k : k + 1, :]) for k in range(4)] * 2, axis=0).astype(BF16)
    behind = jnp.concatenate([onehot_rows(near[6 - k : 7 - k, :]) for k in range(4)] * 2, axis=0).astype(BF16)
    own = onehot_rows(near[3:4, :])
    own2 = jnp.concatenate([own, own], axis=0).astype(BF16)
    upto = jnp.where(iota((length, length), 0) <= iota((length, length), 1), 1.0, 0.0).astype(BF16)
    count = dot(own.astype(BF16), upto)
    before = count - own
    ld = ldt[...]
    full = sum(ld[:, v : v + 1] * count[v : v + 1, :] for v in range(5))
    less = sum(ld[:, v : v + 1] * before[v : v + 1, :] for v in range(5))
    full_t, less_t = jnp.transpose(full), jnp.transpose(less)
    spread = head_spread(2 * heads, 2 * inner, head_dim)
    spread = jnp.concatenate([spread, spread], axis=0).astype(BF16)
    enter = (jnp.exp(full), jnp.exp(full[:, length - 1 : length] - less))
    enter = [jnp.concatenate(split(part), axis=0).astype(BF16) for part in enter]
    row, lane = iota((CHUNK, CHUNK), 0), iota((CHUNK, CHUNK), 1)
    lower, upper = row >= lane, row <= lane
    first_half = iota((CHUNK, CHUNK), 1) < head_dim
    span = lambda i: slice(i * CHUNK, (i + 1) * CHUNK)
    for strand in range(2):
        gate = dot(own2, look[:, strand * inner : (strand + 1) * inner], TN)
        stepx = dot(own2, look[:, (2 + strand) * inner : (3 + strand) * inner], TN)
        values, stepped, scores = [], [], []
        for way, hot in enumerate((ahead, behind)):
            conv = silu(dot(hot, taps[:, strand * width : (strand + 1) * width], TN))
            x = conv[:, :inner]
            keys, read = conv[:, inner : inner + state].astype(BF16), conv[:, inner + state :].astype(BF16)
            reads[2 * strand + way] = read
            values.append(x)
            stepped.append((x * stepx).astype(BF16))
            scores.append(dot(read, keys, NT))
            eg[2 * strand + way] = (
                dot(enter[way], spread[:, strand * inner : (strand + 1) * inner], TN) * gate
            ).astype(BF16)
        cut = {}
        for i in range(blocks):
            for j in range(blocks):
                if i >= j:
                    s = scores[0][span(i), span(j)]
                    cut[0, i, j] = jnp.where(lower, s, 0.0) if i == j else s
                if i <= j:
                    s = scores[1][span(i), span(j)]
                    cut[1, i, j] = jnp.where(upper, s, 0.0) if i == j else s
        for pair in range(heads // 2):
            columns = slice(pair * 2 * head_dim, (pair + 1) * 2 * head_dim)
            found = []
            for head in (2 * pair, 2 * pair + 1):
                k = strand * heads + head
                decay = {}
                for i in range(blocks):
                    for j in range(blocks):
                        if i >= j:
                            down = full_t[span(i), k : k + 1] - full[k : k + 1, span(j)]
                        if i <= j:
                            up = less[k : k + 1, span(j)] - less_t[span(i), k : k + 1]
                        gap = down if i > j else up if i < j else jnp.where(lower, down, up)
                        decay[i, j] = jnp.exp(gap)
                for way in range(2):
                    out = []
                    for i in range(blocks):
                        js = range(i + 1) if way == 0 else range(i, blocks)
                        weights = jnp.concatenate([(cut[way, i, j] * decay[i, j]).astype(BF16) for j in js], axis=1)
                        out.append(dot(weights, stepped[way][js[0] * CHUNK : (js[-1] + 1) * CHUNK, columns]))
                    found.append(out)
            for way in range(2):
                for i in range(blocks):
                    y = jnp.where(first_half, found[way][i], found[2 + way][i])
                    y = y + skipx[:, columns] * values[way][span(i), columns]
                    yg[2 * strand + way, span(i), columns] = y * gate[span(i), columns]


def finish_kernel(
    ids, ldt, stept, stepk, taps, taps_t, xt, bt, reads, yg, eg, norm_gain, w_out,
    out,
    *, heads, head_dim, state,
):
    members, length = ids.shape
    inner = heads * head_dim
    width = inner + 2 * state
    position = lax.axis_index("ctx")
    letters = 5
    every = ids[...]
    lane = iota((members, length), 1)
    block = iota((members, length), 0)
    prev, after = [], []
    up, down = pltpu.roll(every, 1, 0), pltpu.roll(every, members - 1, 0)
    for k in (1, 2, 3):
        inside, outside = pltpu.roll(every, k, 1), pltpu.roll(up, k, 1)
        found = jnp.where(lane >= k, inside, outside)
        prev.append(jnp.where((block == 0) & (lane < k), -1, found))
        inside, outside = pltpu.roll(every, length - k, 1), pltpu.roll(down, length - k, 1)
        found = jnp.where(lane < length - k, inside, outside)
        after.append(jnp.where((block == members - 1) & (lane >= length - k), -1, found))
    code_ahead = jnp.where((block == 0) & (lane < 3), -1, prev[2] * 25 + prev[1] * 5 + prev[0])
    code_behind = jnp.where((block == members - 1) & (lane >= length - 3), -1, after[2] * 25 + after[1] * 5 + after[0])
    code = jnp.where(block < position, code_ahead, code_behind)

    marks = [onehot_rows(every[b : b + 1, :]) for b in range(members)]
    mark = jnp.concatenate(marks, axis=0)
    rows = members * LETTER_ROWS
    its_block = iota((rows, 1), 0) >> 3
    i, j = iota((rows, rows), 0), iota((rows, rows), 1)
    bi, bj = i >> 3, j >> 3
    between = ((bi < bj) & (bj < position)) | ((position < bj) & (bj < bi))
    between = jnp.where(((i & 7) == (j & 7)) & between, 1.0, 0.0).astype(BF16)
    amid = dot(between, mark.astype(BF16)).astype(BF16)
    s, t = iota((length, length), 0), iota((length, length), 1)
    later = jnp.where(s > t, 1.0, 0.0).astype(BF16)
    earlier = jnp.where(s < t, 1.0, 0.0).astype(BF16)
    ones = jnp.ones((length, length), BF16)
    counts = (
        dot(jnp.where(its_block < position, mark, 0.0).astype(BF16), later)
        + dot(jnp.where(its_block > position, mark, 0.0).astype(BF16), earlier)
        + dot(amid, ones)
    )
    ld = ldt[...]
    weighed, hot, far = [], [], {}
    for b in range(members):
        count = counts[b * LETTER_ROWS : (b + 1) * LETTER_ROWS]
        far_b = jnp.exp(sum(ld[:, v : v + 1] * count[v : v + 1, :] for v in range(letters)))
        if b in (0, members - 1):
            far[b] = far_b
        by_last = [far_b * marks[b][v : v + 1, :] for v in range(letters)]
        in_front = jnp.where(b < position, 1.0, 0.0)
        in_back = jnp.where(b > position, 1.0, 0.0)
        by_last = [part * in_front for part in by_last] + [part * in_back for part in by_last]
        weighed.append(jnp.concatenate(by_last, axis=0).astype(BF16))
        hot.append(jnp.where(iota((128, length), 0) == code[b : b + 1, :], 1.0, 0.0).astype(BF16))
    sums = dot(jnp.concatenate(weighed, axis=1), jnp.concatenate(hot, axis=1), NT)

    edge_lane = iota((1, 128), 1)
    tail = slice(length - 128, length)
    digits = [jnp.where(edge_lane < 64, prev[2 - k][0:1, :128], after[2 - k][members - 1 :, tail]) for k in range(3)]
    digits.append(jnp.where(edge_lane < 64, every[0:1, :128], every[members - 1 :, tail]))
    edge_hot = jnp.concatenate([onehot_rows(d) for d in digits] * 2, axis=0).astype(BF16)
    st = stept[...]
    first_step = sum(st[:, v : v + 1] * marks[0][v : v + 1, :128] for v in range(letters))
    last_step = sum(st[:, v : v + 1] * marks[members - 1][v : v + 1, tail] for v in range(letters))
    edge_ahead = jnp.where((edge_lane < 3) & (position > 0), far[0][:, :128] * first_step, 0.0)
    edge_behind = jnp.where(
        (edge_lane >= 125) & (position < members - 1), far[members - 1][:, tail] * last_step, 0.0
    )
    span = 2 * heads
    total = jnp.zeros((length, inner), F32)
    weights = []
    for way, edge in enumerate((edge_ahead, edge_behind)):
        base = way * letters * span
        wide = jnp.concatenate([sums[base + v * span : base + (v + 1) * span] for v in range(letters)], axis=1)
        weights.append(jnp.concatenate([wide * stepk[...], edge], axis=1).astype(BF16))
    for strand in range(2):
        edge_x = silu(dot(taps_t[strand], edge_hot)).astype(BF16)
        edge_b = silu(dot(edge_hot, taps[:, strand * width + inner : strand * width + inner + state], TN)).astype(BF16)
        keys = jnp.concatenate([bt[strand], edge_b], axis=0)
        for way in range(2):
            scaled = []
            for head in range(heads):
                at = slice(head * head_dim, (head + 1) * head_dim)
                x_head = jnp.concatenate([xt[strand, at, :], edge_x[at]], axis=1)
                scaled.append(x_head * weights[way][strand * heads + head : strand * heads + head + 1, :])
            entering = dot(jnp.concatenate(scaled, axis=0), keys).astype(BF16)
            which = 2 * strand + way
            carried = dot(reads[which], entering, NT)
            g = yg[which] + carried * eg[which].astype(F32)
            power = jnp.sum(g * g, axis=1, keepdims=True) * (1.0 / inner)
            total = total + g * lax.rsqrt(power + 1e-05)
    out[...] = dot((total * norm_gain[...]).astype(BF16), w_out[...]).astype(BF16)


def on_device(
    base_ids, complement, embedding, w_gate, w_mix, w_step, step_bias, decay_rate,
    conv_weight, conv_bias, skip_gain, norm_gain, w_out,
):
    length = base_ids.shape[0]
    heads = decay_rate.shape[0]
    inner = w_gate.shape[1]
    head_dim = inner // heads
    width = w_mix.shape[1]
    state = (width - inner) // 2
    members = lax.axis_size("ctx")
    position = lax.axis_index("ctx")
    sizes = dict(heads=heads, head_dim=head_dim, state=state)
    letters = embedding.shape[0]
    codes = letters * 128
    vmem = pl.BlockSpec(memory_space=VMEM)
    params = pltpu.CompilerParams(vmem_limit_bytes=24 * 1024 * 1024)

    odd = position % 2 == 1
    own = base_ids.reshape(1, length)
    across = [(i, (i + 1) % members if i % 2 else (i - 1) % members) for i in range(members)]
    other = lax.ppermute(own, "ctx", across)
    two = jnp.where(odd, jnp.concatenate([own, other]), jnp.concatenate([other, own]))
    got = lax.ppermute(two, "ctx", [(i, i ^ 1) for i in range(members)])
    window = jnp.where(odd, jnp.concatenate([got, two]), jnp.concatenate([two, got]))
    left = jnp.where(odd, window[1:2], window[0:1])[:, length - 3 :]
    right = jnp.where(odd, window[3:4], window[2:3])[:, :3]
    left = jnp.where(position == 0, -1, left)
    right = jnp.where(position == members - 1, -1, right)
    extended = jnp.concatenate([left, own, right, jnp.zeros((1, 1), I32)], axis=1)
    near = jnp.concatenate([extended[:, k : k + length] for k in range(7)] + [own], axis=0)

    bit = 4
    ids = window
    while bit < members:
        got = lax.ppermute(ids, "ctx", [(i, i ^ bit ^ 1) for i in range(members)])
        ids = jnp.where(position & bit == 0, jnp.concatenate([ids, got]), jnp.concatenate([got, ids]))
        bit *= 2
    ids = jnp.where(position & 2 == 0, jnp.roll(ids, -1, axis=0), jnp.roll(ids, 1, axis=0))

    smem = pl.BlockSpec(memory_space=pltpu.SMEM)
    row = lambda a: a.reshape(1, -1)
    shape = jax.ShapeDtypeStruct
    taps, taps_t, look, ldt, stept, stepk, skipx, xt, bt = pl.pallas_call(
        functools.partial(tables_kernel, **sizes),
        out_shape=[
            shape((64, 2 * width), BF16),
            shape((2, inner, 64), BF16),
            shape((2 * LETTER_ROWS, 4 * inner), F32),
            shape((2 * heads, LETTER_ROWS), F32),
            shape((2 * heads, LETTER_ROWS), F32),
            shape((2 * heads, codes), F32),
            shape((1, inner), F32),
            shape((2, inner, codes), BF16),
            shape((2, codes, state), BF16),
        ],
        in_specs=[smem] + [vmem] * 9,
        out_specs=[vmem] * 9,
        scratch_shapes=[VMEM((2 * LETTER_ROWS, embedding.shape[1]), F32)],
        compiler_params=params,
        name="tables",
    )(
        complement, embedding, w_gate, w_mix, w_step, row(step_bias), row(decay_rate), conv_weight,
        row(conv_bias), row(skip_gain),
    )
    look = look.astype(BF16)

    yg, eg, reads = pl.pallas_call(
        functools.partial(local_kernel, **sizes),
        out_shape=[
            shape((4, length, inner), F32),
            shape((4, length, inner), BF16),
            shape((4, length, state), BF16),
        ],
        in_specs=[vmem] * 5,
        out_specs=[vmem] * 3,
        compiler_params=params,
        name="local",
    )(near, taps, look, ldt, skipx)

    return pl.pallas_call(
        functools.partial(finish_kernel, **sizes),
        out_shape=shape((length, w_out.shape[1]), BF16),
        in_specs=[vmem] * 13,
        out_specs=vmem,
        compiler_params=params,
        name="finish",
    )(ids, ldt, stept, stepk, taps, taps_t, xt, bt, reads, yg, eg, row(norm_gain), w_out)


def solution(mesh):
    return jax.shard_map(
        on_device,
        mesh=mesh,
        in_specs=(P(("dp", "ctx")), P(), P(), P(), P(), P(), P(), P(), P(), P(), P(), P(), P()),
        out_specs=P(("dp", "ctx"), None),
        check_vma=False,
    )
```

time: 418 us -> 43.9 us (0.11)
  the two profiles are of different devices: /device:TPU:0 before, /device:TPU:11 now
where the time goes in v1:
time: 43.9 us; the launch traced here: 43.2 us
  local copies, waits for them, and re-layouts  16.3 us (37%)
  Pallas kernels  12.9 us (29%)
  starting transfers between devices  6.83 us (16%)
  waiting for transfers between devices  4.79 us (11%)
  other arithmetic  2.33 us (5%)
    unnamed x37, local copies, waits for them, and re-layouts  14.8 us
    pallas_call x1, Pallas kernels, on_device(): pl.pallas_call(functools.partial(finish_kernel, **sizes), out_shape=shape...  5.86 us
    ppermute x2, starting transfers between devices, on_device(): got = lax.ppermute(ids, 'ctx', [(i, i ^ bit ^ 1) for i in range(members)])  5 us
    pallas_call x1, Pallas kernels, on_device(): pl.pallas_call(functools.partial(local_kernel, **sizes), out_shape=[shape...  4.71 us
    ppermute x2, waiting for transfers between devices, on_device(): got = lax.ppermute(ids, 'ctx', [(i, i ^ bit ^ 1) for i in range(members)])  2.51 us
    pallas_call x1, Pallas kernels, on_device(): pl.pallas_call(functools.partial(tables_kernel, **sizes), out_shape=[shap...  2.34 us
    ppermute x1, waiting for transfers between devices, on_device(): other = lax.ppermute(own, 'ctx', across)  2.27 us
    ppermute x1, starting transfers between devices, on_device(): other = lax.ppermute(own, 'ctx', across)  1.83 us
  transfers between devices with their start and end apart: 4, of which 2 were waited for; matrix products, arithmetic and copies ran while one was open for 9% of the time, Pallas kernels for 16%

profile of v1, /device:TPU:11, one launch (start us, length us, event | category | flops | bytes accessed | tf_op | source)
XLA Modules:
  0.0 43.2 jit_solution(7867023496380007475)
XLA Ops:
  0.0 1.8 %collective-permute-start = (s32[1,256]{1,0:T(1,128)}, s32[1,256]{1,0:T(1,128)S(1)}, u32[]{:S(2)}, u32[]{:S(2)}) collective-permute-start(s32[1,256]{1,0:T(1,128)} %bitcast.9), channel_id=1, source_target_pairs={{0,15},{1,2},{2,1},{3,4},{4,3},{5,6},{6,5},{7,8},{8,7},{9,10},{10,... | collective-permute-start | bytes 3080 | tf_op jit(solution)/shard_map/ppermute | solution.py:312
  1.8 2.3 %collective-permute-done = s32[1,256]{1,0:T(1,128)S(1)} collective-permute-done((s32[1,256]{1,0:T(1,128)}, s32[1,256]{1,0:T(1,128)S(1)}, u32[]{:S(2)}, u32[]{:S(2)}) %collective-permute-start) | collective-permute-done | bytes 1056 | tf_op jit(solution)/shard_map/ppermute | solution.py:312
  4.1 0.8 %add_select_fusion.4 = s32[2,256]{1,0:T(2,128)S(1)} fusion(s32[1,256]{1,0:T(1,128)S(1)} %collective-permute-done, s32[1,256]{1,0:T(1,128)} %bitcast.10, pred[]{:T(512)S(6)} %eq.23), kind=kLoop, calls=%fused_computation.4 | loop fusion | flops 1536 | bytes 4097 | tf_op jit(solution)/shard_map/jit(_where)/select_n | solution.py:313
  4.9 0.7 %reshape.23.norm_gain = f32[1,768]{1,0:T(1,128)S(1)} reshape(f32[768]{0:T(1024)} %param.24) | data formatting | bytes 6144 | tf_op jit(solution)/shard_map/reshape | solution.py:332
  5.6 1.6 %copy.14.w_step = bf16[768,12]{1,0:T(8,128)(2,1)} copy(bf16[768,12]{0,1:T(8,128)(2,1)} %param.18) | data formatting | bytes 36864 | tf_op args[5]
  7.2 1.4 %copy-done = bf16[768,1024]{1,0:T(8,128)(2,1)S(1)} copy-done((bf16[768,1024]{1,0:T(8,128)(2,1)S(1)}, bf16[768,1024]{1,0:T(8,128)(2,1)}, u32[]{:S(2)}) %copy-start) | copy-done | bytes 1572888
  8.6 1.3 %copy-done.2 = bf16[768,768]{1,0:T(8,128)(2,1)S(1)} copy-done((bf16[768,768]{1,0:T(8,128)(2,1)S(1)}, bf16[768,768]{1,0:T(8,128)(2,1)}, u32[]{:S(2)}) %copy-start.2) | copy-done | bytes 1179672
  9.8 0.9 %copy-done.3 = bf16[768,12]{1,0:T(8,128)(2,1)S(1)} copy-done((bf16[768,12]{1,0:T(8,128)(2,1)S(1)}, bf16[768,12]{1,0:T(8,128)(2,1)}, u32[]{:S(2)}) %copy-start.3) | copy-done | bytes 18456
  10.8 0.7 %copy-done.10 = f32[4,1024]{1,0:T(4,128)S(1)} copy-done((f32[4,1024]{1,0:T(4,128)S(1)}, f32[4,1024]{1,0:T(4,128)}, u32[]{:S(2)}) %copy-start.10) | copy-done | bytes 16408
  11.5 0.7 %copy-done.11 = bf16[5,768]{1,0:T(8,128)(2,1)S(1)} copy-done((bf16[5,768]{1,0:T(8,128)(2,1)S(1)}, bf16[5,768]{1,0:T(8,128)(2,1)}, u32[]{:S(2)}) %copy-start.11) | copy-done | bytes 7704
  12.2 0.7 %copy-done.12 = f32[1024]{0:T(1024)S(1)} copy-done((f32[1024]{0:T(1024)S(1)}, f32[1024]{0:T(1024)}, u32[]{:S(2)}) %copy-start.12) | copy-done | bytes 4120
  15.5 2.3 %tables.1 = (bf16[64,2048]{1,0:T(8,128)(2,1)S(1)}, bf16[2,768,64]{2,1,0:T(8,128)(2,1)S(1)}, f32[16,3072]{1,0:T(8,128)S(1)}, f32[24,8]{1,0:T(8,128)S(1)}, f32[24,...) custom-call(s32[5]{0:T(128)S(1)} %copy-done.13, ...), custom_call_target="tpu_custom_call" | custom-call | tf_op jit(solution)/shard_map/tables/pallas_call | solution.py:334
  17.9 0.7 %copy-done.4 = bf16[2,768,64]{2,1,0:T(8,128)(2,1)} copy-done((bf16[2,768,64]{2,1,0:T(8,128)(2,1)}, bf16[2,768,64]{2,1,0:T(8,128)(2,1)S(1)}, u32[]{:S(2)}) %copy-start.4) | copy-done | bytes 196632
  18.6 0.7 %copy-done.6 = bf16[2,640,128]{2,1,0:T(8,128)(2,1)} copy-done((bf16[2,640,128]{2,1,0:T(8,128)(2,1)}, bf16[2,640,128]{2,1,0:T(8,128)(2,1)S(1)}, u32[]{:S(2)}) %copy-start.6) | copy-done | bytes 327704
  20.7 2.5 %collective-permute-done.2 = s32[4,256]{1,0:T(4,128)S(1)} collective-permute-done((s32[4,256]{1,0:T(4,128)S(1)}, s32[4,256]{1,0:T(4,128)S(1)}, u32[]{:S(2)}, u32[]{:S(2)}) %collective-permute-start.2) | collective-permute-done | bytes 4128 | tf_op jit(solution)/shard_map/ppermute | solution.py:326
  23.2 4.4 %collective-permute-start.3 = (s32[8,256]{1,0:T(8,128)S(1)}, s32[8,256]{1,0:T(8,128)}, u32[]{:S(2)}, u32[]{:S(2)}) collective-permute-start(s32[8,256]{1,0:T(8,128)S(1)} %add_select_fusion.2), channel_id=1, source_target_pairs={{0,9},{1,8},{2,11},{3,10},{4,13},{5,12},{6,15},{7,14},{8,1},{9,0},... | collective-permute-start | bytes 24584 | tf_op jit(solution)/shard_map/ppermute | solution.py:326
  27.6 0.7 %pad_add_fusion = (s32[1,256]{1,0:T(1,128)}, s32[1,256]{1,0:T(1,128)}, s32[1,256]{1,0:T(1,128)}, s32[1,256]{1,0:T(1,128)}, s32[1,256]{1,0:T(1,128)}, /*index=5*/s32[1,256]{1,0:T(1,128)}) fusion(s32[1,3]{1,0:T(1,128)S(1)} %get-tuple-element.46, s32[1,256]{1,0:T(1,128)S(1)} %bitcast.13, s32[1,3]{1,0:T(1,128)S(1)} %get-tuple-element.47), kind=kLoop, calls=%fused_computation.17 | loop fusion | flops 1536 | bytes 7192 | tf_op jit(solution)/shard_map/concatenate | solution.py:320
  28.2 0.8 %concatenate.58.near = s32[8,256]{1,0:T(8,128)S(1)} concatenate(s32[1,256]{1,0:T(1,128)} %get-tuple-element.44, s32[1,256]{1,0:T(1,128)} %get-tuple-element.43, s32[1,256]{1,0:T(1,128)} %get-tuple-element.45, s32[1,256]{1,0:T(1,128)} %bitcast.11, s32[1,256]{1,0:T(1,128)} %get-tuple-element.38, s32[1,256]{1,0:T(1,128)} %get-tuple-element.39, s32[1,256]{1,0:T(1,128)} %get-tuple-element.37, ...), dimensions={0} | concatenate | bytes 16384 | tf_op jit(solution)/shard_map/concatenate | solution.py:321
  29.0 4.7 %local.1 = (f32[4,256,768]{2,1,0:T(8,128)S(1)}, bf16[4,256,768]{2,1,0:T(8,128)(2,1)S(1)}, bf16[4,256,128]{2,1,0:T(8,128)(2,1)S(1)}) custom-call(s32[8,256]{1,0:T(8,128)S(1)} %concatenate.58.near, bf16[64,2048]{1,0:T(8,128)(2,1)S(1)} %get-tuple-element.20.taps, bf16[16,3072]{1,0:T(8,128)(2,1)S(1)} %convert_element_type.3.look, ...), custom_call_target="tpu_custom_call" | custom-call | tf_op jit(solution)/shard_map/local/pallas_call | solution.py:358
  33.8 0.8 %add_select_fusion = s32[16,256]{1,0:T(8,128)S(1)} fusion(s32[8,256]{1,0:T(8,128)} %collective-permute-done.3, s32[8,256]{1,0:T(8,128)S(1)} %add_select_fusion.2, pred[]{:T(512)S(6)} %eq.21), kind=kLoop, calls=%fused_computation | loop fusion | flops 12288 | bytes 32769 | tf_op jit(solution)/shard_map/jit(_where)/select_n | solution.py:327
  34.6 1.0 %copy-done.5 = bf16[2,768,64]{2,1,0:T(8,128)(2,1)S(1)} copy-done((bf16[2,768,64]{2,1,0:T(8,128)(2,1)S(1)}, bf16[2,768,64]{2,1,0:T(8,128)(2,1)}, u32[]{:S(2)}) %copy-start.5) | copy-done | bytes 196632
  35.6 1.0 %copy-done.7 = bf16[2,640,128]{2,1,0:T(8,128)(2,1)S(1)} copy-done((bf16[2,640,128]{2,1,0:T(8,128)(2,1)S(1)}, bf16[2,640,128]{2,1,0:T(8,128)(2,1)}, u32[]{:S(2)}) %copy-start.7) | copy-done | bytes 327704
  36.6 0.8 %copy-done.9 = f32[24,640]{1,0:T(8,128)S(1)} copy-done((f32[24,640]{1,0:T(8,128)S(1)}, f32[24,640]{1,0:T(8,128)}, u32[]{:S(2)}) %copy-start.9) | copy-done | bytes 61464
  37.4 5.9 %finish.1 = bf16[256,768]{1,0:T(8,128)(2,1)} custom-call(s32[16,256]{1,0:T(8,128)S(1)} %add_select_fusion.1.ids, f32[24,8]{1,0:T(8,128)S(1)} %get-tuple-element.17.ldt, f32[24,8]{1,0:T(8,128)S(1)} %get-tuple-element.18.stept, f32[24,640]{1,0:T(8,128)S(1)} %copy-done.9, bf16[64,2048]{1,0:T(8,128)(2,1)S(1)} %get-tuple-element.20.taps, ...), custom_call_target="tpu_custom_call" | custom-call | tf_op jit(solution)/shard_map/finish/pallas_call | solution.py:371
  (37 shorter events, 4.0 us)
Async XLA Ops:
  0.0 4.1 %collective-permute-start = (s32[1,256]{1,0:T(1,128)}, s32[1,256]{1,0:T(1,128)S(1)}, u32[]{:S(2)}, u32[]{:S(2)}) collective-permute-start(s32[1,256]{1,0:T(1,128)} %bitcast.9), channel_id=1, source_target_pairs={{0,15},{1,2},{2,1},{3,4},{4,3},{5,6},{6,5},{7,8},{8,7},{9,10},{10,... | collective-permute-start | bytes 3080 | tf_op jit(solution)/shard_map/ppermute | solution.py:312
  4.9 15.1 %collective-permute-start.1 = (s32[2,256]{1,0:T(2,128)S(1)}, s32[2,256]{1,0:T(2,128)S(1)}, u32[]{:S(2)}, u32[]{:S(2)}) collective-permute-start(s32[2,256]{1,0:T(2,128)S(1)} %add_select_fusion.4), channel_id=1, source_target_pairs={{0,1},{1,0},{2,3},{3,2},{4,5},{5,4},{6,7},{7,6},{8,9},{9,8},{10,11... | collective-permute-start | bytes 6152 | tf_op jit(solution)/shard_map/ppermute | solution.py:314
  7.1 1.4 %copy-start = (bf16[768,1024]{1,0:T(8,128)(2,1)S(1)}, bf16[768,1024]{1,0:T(8,128)(2,1)}, u32[]{:S(2)}) copy-start(bf16[768,1024]{1,0:T(8,128)(2,1)} %w_mix.1) | copy-start | bytes 4718596
  8.6 1.3 %copy-start.2 = (bf16[768,768]{1,0:T(8,128)(2,1)S(1)}, bf16[768,768]{1,0:T(8,128)(2,1)}, u32[]{:S(2)}) copy-start(bf16[768,768]{1,0:T(8,128)(2,1)} %w_gate.1) | copy-start | bytes 3538948
  9.8 0.9 %copy-start.3 = (bf16[768,12]{1,0:T(8,128)(2,1)S(1)}, bf16[768,12]{1,0:T(8,128)(2,1)}, u32[]{:S(2)}) copy-start(bf16[768,12]{1,0:T(8,128)(2,1)} %copy.14.w_step) | copy-start | bytes 55300
  10.8 0.7 %copy-start.10 = (f32[4,1024]{1,0:T(4,128)S(1)}, f32[4,1024]{1,0:T(4,128)}, u32[]{:S(2)}) copy-start(f32[4,1024]{1,0:T(4,128)} %conv_w.1) | copy-start | bytes 49156
  11.5 0.7 %copy-start.11 = (bf16[5,768]{1,0:T(8,128)(2,1)S(1)}, bf16[5,768]{1,0:T(8,128)(2,1)}, u32[]{:S(2)}) copy-start(bf16[5,768]{1,0:T(8,128)(2,1)} %emb.1) | copy-start | bytes 23044
  12.2 0.7 %copy-start.12 = (f32[1024]{0:T(1024)S(1)}, f32[1024]{0:T(1024)}, u32[]{:S(2)}) copy-start(f32[1024]{0:T(1024)} %param.22) | copy-start | bytes 12292
  12.9 0.7 %copy-start.13 = (s32[5]{0:T(128)S(1)}, s32[5]{0:T(128)}, u32[]{:S(2)}) copy-start(s32[5]{0:T(128)} %comp.1) | copy-start | bytes 64
  13.5 0.7 %copy-start.14 = (f32[12]{0:T(128)S(1)}, f32[12]{0:T(128)}, u32[]{:S(2)}) copy-start(f32[12]{0:T(128)} %param.19) | copy-start | bytes 148
  14.2 0.7 %copy-start.15 = (f32[12]{0:T(128)S(1)}, f32[12]{0:T(128)}, u32[]{:S(2)}) copy-start(f32[12]{0:T(128)} %param.20) | copy-start | bytes 148
  14.8 0.7 %copy-start.16 = (f32[12]{0:T(128)S(1)}, f32[12]{0:T(128)}, u32[]{:S(2)}) copy-start(f32[12]{0:T(128)} %param.23) | copy-start | bytes 148
  15.5 12.1 %copy-start.17 = (s32[256]{0:T(256)S(1)}, s32[256]{0:T(256)}, u32[]{:S(2)}) copy-start(s32[256]{0:T(256)} %param.13) | copy-start | bytes 3076
  15.5 19.1 %copy-start.1 = (bf16[768,768]{1,0:T(8,128)(2,1)S(1)}, bf16[768,768]{1,0:T(8,128)(2,1)}, u32[]{:S(2)}) copy-start(bf16[768,768]{1,0:T(8,128)(2,1)} %w_out.1) | copy-start | bytes 3538948
  17.8 0.7 %copy-start.4 = (bf16[2,768,64]{2,1,0:T(8,128)(2,1)}, bf16[2,768,64]{2,1,0:T(8,128)(2,1)S(1)}, u32[]{:S(2)}) copy-start(bf16[2,768,64]{2,1,0:T(8,128)(2,1)S(1)} %get-tuple-element.21.taps_t) | copy-start | bytes 589828
  18.6 0.7 %copy-start.6 = (bf16[2,640,128]{2,1,0:T(8,128)(2,1)}, bf16[2,640,128]{2,1,0:T(8,128)(2,1)S(1)}, u32[]{:S(2)}) copy-start(bf16[2,640,128]{2,1,0:T(8,128)(2,1)S(1)} %get-tuple-element.23.bt) | copy-start | bytes 983044
  19.3 0.6 %copy-start.8 = (f32[24,640]{1,0:T(8,128)}, f32[24,640]{1,0:T(8,128)S(1)}, u32[]{:S(2)}) copy-start(f32[24,640]{1,0:T(8,128)S(1)} %get-tuple-element.19.stepk) | copy-start | bytes 184324
  20.0 3.2 %collective-permute-start.2 = (s32[4,256]{1,0:T(4,128)S(1)}, s32[4,256]{1,0:T(4,128)S(1)}, u32[]{:S(2)}, u32[]{:S(2)}) collective-permute-start(s32[4,256]{1,0:T(4,128)S(1)} %add_select_fusion.3), channel_id=1, source_target_pairs={{0,5},{1,4},{2,7},{3,6},{4,1},{5,0},{6,3},{7,2},{8,13},{9,12},{10,... | collective-permute-start | bytes 12296 | tf_op jit(solution)/shard_map/ppermute | solution.py:326
  23.2 10.6 %collective-permute-start.3 = (s32[8,256]{1,0:T(8,128)S(1)}, s32[8,256]{1,0:T(8,128)}, u32[]{:S(2)}, u32[]{:S(2)}) collective-permute-start(s32[8,256]{1,0:T(8,128)S(1)} %add_select_fusion.2), channel_id=1, source_target_pairs={{0,9},{1,8},{2,11},{3,10},{4,13},{5,12},{6,15},{7,14},{8,1},{9,0},... | collective-permute-start | bytes 24584 | tf_op jit(solution)/shard_map/ppermute | solution.py:326
  34.6 1.0 %copy-start.5 = (bf16[2,768,64]{2,1,0:T(8,128)(2,1)S(1)}, bf16[2,768,64]{2,1,0:T(8,128)(2,1)}, u32[]{:S(2)}) copy-start(bf16[2,768,64]{2,1,0:T(8,128)(2,1)} %copy-done.4) | copy-start | bytes 589828
  35.6 1.0 %copy-start.7 = (bf16[2,640,128]{2,1,0:T(8,128)(2,1)S(1)}, bf16[2,640,128]{2,1,0:T(8,128)(2,1)}, u32[]{:S(2)}) copy-start(bf16[2,640,128]{2,1,0:T(8,128)(2,1)} %copy-done.6) | copy-start | bytes 983044
  36.6 0.8 %copy-start.9 = (f32[24,640]{1,0:T(8,128)S(1)}, f32[24,640]{1,0:T(8,128)}, u32[]{:S(2)}) copy-start(f32[24,640]{1,0:T(8,128)} %copy-done.8) | copy-start | bytes 184324

commit v2 on v1

v2 whole, which is shorter than its diff:
```python
import functools

import jax
import jax.numpy as jnp
from jax import lax
from jax.experimental import pallas as pl
from jax.experimental.pallas import tpu as pltpu
from jax.sharding import PartitionSpec as P

F32, BF16, I32 = jnp.float32, jnp.bfloat16, jnp.int32
LETTER_ROWS = 8
CHUNK = 128
VMEM = pltpu.VMEM
VMEM_LIMIT = 24 * 1024 * 1024
DECAY_AT, STEP_AT, GAIN_AT = 768, 896, 32


def dot(a, b, contract=((1,), (0,))):
    return lax.dot_general(a, b, (contract, ((), ())), preferred_element_type=F32)


TN = ((0,), (0,))
NT = ((1,), (1,))


def silu(x):
    half = 0.5 * x
    return half + half * jnp.tanh(half)


def split(x):
    high = x.astype(BF16).astype(F32)
    return high, x - high


def iota(shape, dim):
    return lax.broadcasted_iota(I32, shape, dim)


def onehot_rows(row):
    return jnp.where(jnp.broadcast_to(row, (LETTER_ROWS, row.shape[1])) == iota((LETTER_ROWS, row.shape[1]), 0), 1.0, 0.0)


def code_onehot(shape, code_dim):
    code, slot = iota(shape, code_dim), iota(shape, 1 - code_dim) & 31
    before, last = code & 127, code >> 7
    first = (before * 41) >> 10
    pair = (before * 205) >> 10
    second, third = pair - 5 * first, before - 5 * pair
    tap = slot >> 3
    digit = jnp.where(tap == 0, first, jnp.where(tap == 1, second, jnp.where(tap == 2, third, last)))
    return jnp.where(digit == (slot & 7), 1.0, 0.0).astype(BF16)


def head_spread(rows, columns, head_dim):
    low = iota((rows, columns), 0) * head_dim
    lane = iota((rows, columns), 1)
    return jnp.where((lane >= low) & (lane < low + head_dim), 1.0, 0.0)


def tables_kernel(
    base_ids_h, comp_h, emb_h, w_gate_h, w_mix_h, w_step_h, step_bias_h, rate_h, conv_w_h, conv_b_h, skip_h,
    norm_gain_h,
    own, wide, xt, small,
    e16, ids_v, comp, emb, w_gate, w_mix, w_step, step_bias, rate, conv_w, conv_b, skip, gain_v, sems,
    *, heads, head_dim, state,
):
    pairs = [
        (emb_h, emb), (comp_h, comp), (w_mix_h, w_mix), (w_step_h, w_step), (step_bias_h, step_bias), (rate_h, rate),
        (skip_h, skip), (conv_w_h, conv_w), (conv_b_h, conv_b), (w_gate_h, w_gate), (base_ids_h, ids_v),
        (norm_gain_h, gain_v),
    ]
    copies = [pltpu.make_async_copy(a, b, sems.at[n]) for n, (a, b) in enumerate(pairs)]
    for copy in copies:
        copy.start()
    letters, inner = emb.shape[0], heads * head_dim
    e16[...] = jnp.zeros_like(e16)
    copies[0].wait()
    copies[1].wait()
    e16[0:letters, :] = emb[...].astype(F32)
    for v in range(letters):
        e16[LETTER_ROWS + v : LETTER_ROWS + v + 1, :] = e16[pl.ds(comp[v], 1), :]
    rows = e16[...].astype(BF16)
    for copy in copies[2:9]:
        copy.wait()
    mix = dot(rows, w_mix[...]).astype(BF16).astype(F32)
    raw = dot(rows, w_step[...], NT) + step_bias[...].reshape(1, heads)
    step = jnp.maximum(raw, 0.0) + jnp.log1p(jnp.exp(-jnp.abs(raw)))
    decay_t = jnp.transpose(-step * rate[...].reshape(1, heads))
    step_t = jnp.transpose(step)
    for strand in range(2):
        at = slice(strand * LETTER_ROWS, (strand + 1) * LETTER_ROWS)
        small[strand * heads : (strand + 1) * heads, DECAY_AT : DECAY_AT + LETTER_ROWS] = decay_t[:, at]
        small[strand * heads : (strand + 1) * heads, STEP_AT : STEP_AT + LETTER_ROWS] = step_t[:, at]
        for v in range(letters):
            small[strand * heads : (strand + 1) * heads, v * 128 : (v + 1) * 128] = jnp.broadcast_to(
                step_t[:, strand * LETTER_ROWS + v : strand * LETTER_ROWS + v + 1], (heads, 128)
            )
    spread = head_spread(heads, inner, head_dim).astype(BF16)
    steps = [dot(part.astype(BF16), spread) for part in split(step)]
    skip_high, skip_rest = split(skip[...].reshape(1, heads))
    skip_mid, skip_low = split(skip_rest)
    small[2 * heads : 2 * heads + 1, :inner] = sum(dot(part.astype(BF16), spread) for part in (skip_high, skip_mid, skip_low))
    width, codes = conv_w.shape[1], xt.shape[2]
    by_column = code_onehot((64, codes), 1)
    for strand in range(2):
        letter_rows = mix[strand * LETTER_ROWS : (strand + 1) * LETTER_ROWS]
        weighted = [conv_w[k : k + 1, :] * letter_rows for k in range(4)]
        weighted[3] = weighted[3] + conv_b[...].reshape(1, -1)
        high, low = split(jnp.concatenate(weighted, axis=0))
        both = jnp.concatenate([high, low], axis=0)
        wide[strand, :, :width] = both.astype(BF16)
        across = jnp.transpose(both[:, : inner + state]).astype(BF16)
        for low_row in range(0, inner + state, CHUNK):
            xt[strand, low_row : low_row + CHUNK, :] = silu(dot(across[low_row : low_row + CHUNK], by_column)).astype(BF16)
    copies[9].wait()
    gate = silu(dot(rows, w_gate[...]).astype(BF16).astype(F32))
    gates = split(gate)
    for strand in range(2):
        at = slice(strand * LETTER_ROWS, (strand + 1) * LETTER_ROWS)
        rest = jnp.zeros((3 * LETTER_ROWS, 2 * inner), F32)
        parts = [jnp.concatenate([gates[n][at], steps[n][at]], axis=1) for n in range(2)]
        wide[strand, :, width:] = jnp.concatenate([rest, parts[0], rest, parts[1]], axis=0).astype(BF16)
    for copy in copies[10:]:
        copy.wait()
    own[...] = ids_v[...].reshape(own.shape)
    small[GAIN_AT : GAIN_AT + 1, :inner] = gain_v[...].reshape(1, inner)


def local_kernel(
    window, wide, small, *rest,
    strand, heads, head_dim, state,
):
    yg, eg, reads = rest[-3:]
    length, inner = window.shape[1], heads * head_dim
    blocks = length // CHUNK
    members, position = lax.axis_size("ctx"), lax.axis_index("ctx")
    odd = position % 2 == 1
    here = jnp.where(odd, window[2:3, :], window[1:2, :])
    back = jnp.where(position == 0, -1, jnp.where(odd, window[1:2, :], window[0:1, :]))
    fore = jnp.where(position == members - 1, -1, jnp.where(odd, window[3:4, :], window[2:3, :]))
    place = iota((1, length), 1)
    rows_behind, rows_ahead = [here], [here]
    for k in (1, 2, 3):
        rows_behind.append(jnp.where(place >= k, pltpu.roll(here, k, 1), pltpu.roll(back, k, 1)))
        rows_ahead.append(
            jnp.where(place < length - k, pltpu.roll(here, length - k, 1), pltpu.roll(fore, length - k, 1))
        )
    ahead = jnp.concatenate([onehot_rows(r) for r in rows_behind[::-1]] * 2, axis=0).astype(BF16)
    behind = jnp.concatenate([onehot_rows(r) for r in rows_ahead[::-1]] * 2, axis=0).astype(BF16)
    own = onehot_rows(here)
    upto = jnp.where(iota((length, length), 0) <= iota((length, length), 1), 1.0, 0.0).astype(BF16)
    count = dot(own.astype(BF16), upto)
    before = count - own
    ld = small[strand * heads : (strand + 1) * heads, DECAY_AT : DECAY_AT + LETTER_ROWS]
    skipx = small[2 * heads : 2 * heads + 1, :inner]
    width = inner + 2 * state
    full = sum(ld[:, v : v + 1] * count[v : v + 1, :] for v in range(5))
    less = sum(ld[:, v : v + 1] * before[v : v + 1, :] for v in range(5))
    full_t, less_t = jnp.transpose(full), jnp.transpose(less)
    spread = head_spread(heads, inner, head_dim)
    spread = spread.astype(BF16)
    enter = (jnp.exp(full), jnp.exp(full[:, length - 1 : length] - less))
    enter = [[half.astype(BF16) for half in split(part)] for part in enter]
    row, lane = iota((CHUNK, CHUNK), 0), iota((CHUNK, CHUNK), 1)
    lower, upper = row >= lane, row <= lane
    first_half = iota((CHUNK, CHUNK), 1) < head_dim
    span = lambda i: slice(i * CHUNK, (i + 1) * CHUNK)
    gate = dot(ahead, wide[strand, :, width : width + inner], TN)
    stepx = dot(ahead, wide[strand, :, width + inner :], TN)
    values, stepped, scores = [], [], []
    for way, hot in enumerate((ahead, behind)):
        conv = silu(dot(hot, wide[strand, :, :width], TN))
        x = conv[:, :inner]
        keys, read = conv[:, inner : inner + state].astype(BF16), conv[:, inner + state :].astype(BF16)
        reads[way] = read
        values.append(x)
        stepped.append((x * stepx).astype(BF16))
        scores.append(dot(read, keys, NT))
        eg[way] = (
            sum(dot(half, spread, TN) for half in enter[way]) * gate
        ).astype(BF16)
    cut = {}
    for i in range(blocks):
        for j in range(blocks):
            if i >= j:
                s = scores[0][span(i), span(j)]
                cut[0, i, j] = jnp.where(lower, s, 0.0) if i == j else s
            if i <= j:
                s = scores[1][span(i), span(j)]
                cut[1, i, j] = jnp.where(upper, s, 0.0) if i == j else s
    for pair in range(heads // 2):
        columns = slice(pair * 2 * head_dim, (pair + 1) * 2 * head_dim)
        found = []
        for head in (2 * pair, 2 * pair + 1):
            k = head
            decay = {}
            for i in range(blocks):
                for j in range(blocks):
                    if i >= j:
                        down = full_t[span(i), k : k + 1] - full[k : k + 1, span(j)]
                    if i <= j:
                        up = less[k : k + 1, span(j)] - less_t[span(i), k : k + 1]
                    gap = down if i > j else up if i < j else jnp.where(lower, down, up)
                    decay[i, j] = jnp.exp(gap)
            for way in range(2):
                out = []
                for i in range(blocks):
                    js = range(i + 1) if way == 0 else range(i, blocks)
                    weights = jnp.concatenate([(cut[way, i, j] * decay[i, j]).astype(BF16) for j in js], axis=1)
                    out.append(dot(weights, stepped[way][js[0] * CHUNK : (js[-1] + 1) * CHUNK, columns]))
                found.append(out)
        for way in range(2):
            for i in range(blocks):
                y = jnp.where(first_half, found[way][i], found[2 + way][i])
                y = y + skipx[:, columns] * values[way][span(i), columns]
                yg[way, span(i), columns] = y * gate[span(i), columns]


def finish_kernel(
    ids, wide, xt, small, reads0, yg0, eg0, reads1, yg1, eg1, w_out_h,
    out,
    w_out, sem,
    *, heads, head_dim, state,
):
    members, length = ids.shape
    inner = heads * head_dim
    position = lax.axis_index("ctx")
    letters = 5
    load = pltpu.make_async_copy(w_out_h, w_out, sem)
    load.start()
    every = ids[...]
    lane = iota((members, length), 1)
    block = iota((members, length), 0)
    prev, after = [], []
    up, down = pltpu.roll(every, 1, 0), pltpu.roll(every, members - 1, 0)
    for k in (1, 2, 3):
        inside, outside = pltpu.roll(every, k, 1), pltpu.roll(up, k, 1)
        found = jnp.where(lane >= k, inside, outside)
        prev.append(jnp.where((block == 0) & (lane < k), -1, found))
        inside, outside = pltpu.roll(every, length - k, 1), pltpu.roll(down, length - k, 1)
        found = jnp.where(lane < length - k, inside, outside)
        after.append(jnp.where((block == members - 1) & (lane >= length - k), -1, found))
    code_ahead = jnp.where((block == 0) & (lane < 3), -1, prev[2] * 25 + prev[1] * 5 + prev[0])
    code_behind = jnp.where((block == members - 1) & (lane >= length - 3), -1, after[2] * 25 + after[1] * 5 + after[0])
    code = jnp.where(block < position, code_ahead, code_behind)

    marks = [onehot_rows(every[b : b + 1, :]) for b in range(members)]
    mark = jnp.concatenate(marks, axis=0)
    rows = members * LETTER_ROWS
    its_block = iota((rows, 1), 0) >> 3
    i, j = iota((rows, rows), 0), iota((rows, rows), 1)
    bi, bj = i >> 3, j >> 3
    between = ((bi < bj) & (bj < position)) | ((position < bj) & (bj < bi))
    between = jnp.where(((i & 7) == (j & 7)) & between, 1.0, 0.0).astype(BF16)
    amid = dot(between, mark.astype(BF16)).astype(BF16)
    s, t = iota((length, length), 0), iota((length, length), 1)
    later = jnp.where(s > t, 1.0, 0.0).astype(BF16)
    earlier = jnp.where(s < t, 1.0, 0.0).astype(BF16)
    ones = jnp.ones((length, length), BF16)
    counts = (
        dot(jnp.where(its_block < position, mark, 0.0).astype(BF16), later)
        + dot(jnp.where(its_block > position, mark, 0.0).astype(BF16), earlier)
        + dot(amid, ones)
    )
    ld = small[: 2 * heads, DECAY_AT : DECAY_AT + LETTER_ROWS]
    weighed, hot, far = [], [], {}
    for b in range(members):
        count = counts[b * LETTER_ROWS : (b + 1) * LETTER_ROWS]
        far_b = jnp.exp(sum(ld[:, v : v + 1] * count[v : v + 1, :] for v in range(letters)))
        if b in (0, members - 1):
            far[b] = far_b
        by_last = [far_b * marks[b][v : v + 1, :] for v in range(letters)]
        in_front = jnp.where(b < position, 1.0, 0.0)
        in_back = jnp.where(b > position, 1.0, 0.0)
        by_last = [part * in_front for part in by_last] + [part * in_back for part in by_last]
        weighed.append(jnp.concatenate(by_last, axis=0).astype(BF16))
        hot.append(jnp.where(iota((128, length), 0) == code[b : b + 1, :], 1.0, 0.0).astype(BF16))
    sums = dot(jnp.concatenate(weighed, axis=1), jnp.concatenate(hot, axis=1), NT)

    edge_lane = iota((1, 128), 1)
    tail = slice(length - 128, length)
    digits = [jnp.where(edge_lane < 64, prev[2 - k][0:1, :128], after[2 - k][members - 1 :, tail]) for k in range(3)]
    digits.append(jnp.where(edge_lane < 64, every[0:1, :128], every[members - 1 :, tail]))
    edge_hot = jnp.concatenate([onehot_rows(d) for d in digits] * 2, axis=0).astype(BF16)
    st = small[: 2 * heads, STEP_AT : STEP_AT + LETTER_ROWS]
    stepk = small[: 2 * heads, : letters * 128]
    first_step = sum(st[:, v : v + 1] * marks[0][v : v + 1, :128] for v in range(letters))
    last_step = sum(st[:, v : v + 1] * marks[members - 1][v : v + 1, tail] for v in range(letters))
    edge_ahead = jnp.where((edge_lane < 3) & (position > 0), far[0][:, :128] * first_step, 0.0)
    edge_behind = jnp.where(
        (edge_lane >= 125) & (position < members - 1), far[members - 1][:, tail] * last_step, 0.0
    )
    span = 2 * heads
    total = jnp.zeros((length, inner), F32)
    weights = []
    for way, edge in enumerate((edge_ahead, edge_behind)):
        base = way * letters * span
        by_code = jnp.concatenate([sums[base + v * span : base + (v + 1) * span] for v in range(letters)], axis=1)
        weights.append(jnp.concatenate([by_code * stepk, edge], axis=1).astype(BF16))
    for strand in range(2):
        edge = silu(dot(wide[strand, :, : inner + state], edge_hot, TN)).astype(BF16)
        keys = jnp.concatenate([xt[strand, inner:, :], edge[inner:]], axis=1)
        for way in range(2):
            scaled = []
            for head in range(heads):
                at = slice(head * head_dim, (head + 1) * head_dim)
                x_head = jnp.concatenate([xt[strand, at, :], edge[at]], axis=1)
                scaled.append(x_head * weights[way][strand * heads + head : strand * heads + head + 1, :])
            entering = dot(jnp.concatenate(scaled, axis=0), keys, NT).astype(BF16)
            reads, yg, eg = ((reads0, yg0, eg0), (reads1, yg1, eg1))[strand]
            carried = dot(reads[way], entering, NT)
            g = yg[way] + carried * eg[way].astype(F32)
            power = jnp.sum(g * g, axis=1, keepdims=True) * (1.0 / inner)
            total = total + g * lax.rsqrt(power + 1e-05)
    load.wait()
    out[...] = dot((total * small[GAIN_AT : GAIN_AT + 1, :inner]).astype(BF16), w_out[...]).astype(BF16)


def on_device(
    base_ids, complement, embedding, w_gate, w_mix, w_step, step_bias, decay_rate,
    conv_weight, conv_bias, skip_gain, norm_gain, w_out,
):
    length = base_ids.shape[0]
    heads = decay_rate.shape[0]
    depth, inner = w_gate.shape
    head_dim = inner // heads
    width = w_mix.shape[1]
    state = (width - inner) // 2
    members = lax.axis_size("ctx")
    position = lax.axis_index("ctx")
    sizes = dict(heads=heads, head_dim=head_dim, state=state)
    letters = embedding.shape[0]
    codes = letters * 128
    vmem = pl.BlockSpec(memory_space=VMEM)
    hbm = pl.BlockSpec(memory_space=pltpu.HBM)
    params = pltpu.CompilerParams(vmem_limit_bytes=VMEM_LIMIT)
    held = lambda a: pltpu.with_memory_space_constraint(a, VMEM)
    outside = lambda a: pltpu.with_memory_space_constraint(a, pltpu.HBM)
    shape = VMEM

    odd = position % 2 == 1
    across = [(i, (i + 1) % members if i % 2 else (i - 1) % members) for i in range(members)]
    other = lax.ppermute(base_ids, "ctx", across).reshape(1, length)

    given = (
        base_ids, complement, embedding, w_gate, w_mix, w_step.T, step_bias, decay_rate, conv_weight, conv_bias,
        skip_gain, norm_gain,
    )
    own, wide, xt, small = pl.pallas_call(
        functools.partial(tables_kernel, **sizes),
        out_shape=[
            shape((1, length), I32),
            shape((2, 64, width + 2 * inner), BF16),
            shape((2, inner + state, codes), BF16),
            shape((40, 1024), F32),
        ],
        in_specs=[hbm] * len(given),
        out_specs=[vmem] * 4,
        scratch_shapes=[
            VMEM((2 * LETTER_ROWS, depth), F32),
            VMEM(base_ids.shape, I32),
            pltpu.SMEM(complement.shape, I32),
        ]
        + [VMEM(a.shape, a.dtype) for a in given[2:12]]
        + [pltpu.SemaphoreType.DMA((len(given),))],
        compiler_params=params,
        name="tables",
    )(*[outside(a) for a in given])

    two = jnp.where(odd, jnp.concatenate([own, other]), jnp.concatenate([other, own]))
    got = lax.ppermute(two, "ctx", [(i, i ^ 1) for i in range(members)])
    window = jnp.where(odd, jnp.concatenate([got, two]), jnp.concatenate([two, got]))

    def local(strand, *after):
        return pl.pallas_call(
            functools.partial(local_kernel, strand=strand, **sizes),
            out_shape=[
                shape((2, length, inner), F32),
                shape((2, length, inner), BF16),
                shape((2, length, state), BF16),
            ],
            in_specs=[vmem] * (3 + len(after)),
            out_specs=[vmem] * 3,
            compiler_params=params,
            cost_estimate=pl.CostEstimate(flops=4_000_000_000, bytes_accessed=0, transcendentals=0),
            name="local",
        )(*[held(a) for a in (window, wide, small, *after)])

    bit = 4
    ids = window
    strands = []
    while bit < members:
        got = lax.ppermute(ids, "ctx", [(i, i ^ bit ^ 1) for i in range(members)])
        if len(strands) < 2:
            strands.append(local(len(strands), *([] if bit == 4 else [ids])))
        ids = jnp.where(position & bit == 0, jnp.concatenate([ids, got]), jnp.concatenate([got, ids]))
        bit *= 2
    while len(strands) < 2:
        strands.append(local(len(strands)))
    ids = jnp.where(position & 2 == 0, jnp.roll(ids, -1, axis=0), jnp.roll(ids, 1, axis=0))

    (yg0, eg0, reads0), (yg1, eg1, reads1) = strands
    return pl.pallas_call(
        functools.partial(finish_kernel, **sizes),
        out_shape=jax.ShapeDtypeStruct((length, w_out.shape[1]), BF16),
        in_specs=[vmem] * 10 + [hbm],
        out_specs=vmem,
        scratch_shapes=[VMEM(w_out.shape, BF16), pltpu.SemaphoreType.DMA(())],
        compiler_params=params,
        name="finish",
    )(*[held(a) for a in (ids, wide, xt, small, reads0, yg0, eg0, reads1, yg1, eg1)], outside(w_out))


def solution(mesh):
    return jax.shard_map(
        on_device,
        mesh=mesh,
        in_specs=(P(("dp", "ctx")), P(), P(), P(), P(), P(), P(), P(), P(), P(), P(), P(), P()),
        out_specs=P(("dp", "ctx"), None),
        check_vma=False,
    )
```

time: 43.9 us -> 24.7 us (0.56)
  the two profiles are of different devices: /device:TPU:11 before, /device:TPU:0 now
where the time goes in v2:
time: 24.7 us; the launch traced here: 24.5 us
  Pallas kernels  16.2 us (66%)
  starting transfers between devices  6.51 us (26%)
  waiting for transfers between devices  1.57 us (6%)
    pallas_call x1, Pallas kernels, on_device(): pl.pallas_call(functools.partial(finish_kernel, **sizes), out_shape=jax.S...  7.2 us
    pallas_call x2, Pallas kernels, local(): pl.pallas_call(functools.partial(local_kernel, strand=strand, **sizes), o...  5.54 us
    ppermute x1, starting transfers between devices, on_device(): other = lax.ppermute(base_ids, 'ctx', across).reshape(1, length)  5.42 us
    pallas_call x1, Pallas kernels, on_device(): pl.pallas_call(functools.partial(tables_kernel, **sizes), out_shape=[shap...  3.5 us
    ppermute x1, waiting for transfers between devices, on_device(): got = lax.ppermute(two, 'ctx', [(i, i ^ 1) for i in range(members)])  1.13 us
    ppermute x2, starting transfers between devices, on_device(): got = lax.ppermute(ids, 'ctx', [(i, i ^ bit ^ 1) for i in range(members)])  1.02 us
  transfers between devices with their start and end apart: 4, of which 3 were waited for; matrix products, arithmetic and copies ran while one was open for 0% of the time, Pallas kernels for 37%

profile of v2, /device:TPU:0, one launch (start us, length us, event | category | flops | bytes accessed | tf_op | source)
XLA Modules:
  0.0 24.5 jit_solution(16087308967596150422)
XLA Ops:
  0.0 5.4 %collective-permute-start = (s32[256]{0:T(256)}, s32[256]{0:T(256)S(1)}, u32[]{:S(2)}, u32[]{:S(2)}) collective-permute-start(s32[256]{0:T(256)} %base_ids_h.1), channel_id=1, source_target_pairs={{0,15},{1,2},{2,1},{3,4},{4,3},{5,6},{6,5},{7,8},{8,7},{9,10},{10,... | collective-permute-start | bytes 3080 | tf_op jit(solution)/shard_map/ppermute | solution.py:344
  5.4 3.5 %tables.1 = (s32[1,256]{1,0:T(1,128)S(1)}, bf16[2,64,2560]{2,1,0:T(8,128)(2,1)S(1)}, bf16[2,896,640]{2,1,0:T(8,128)(2,1)S(1)}, f32[40,1024]{1,0:T(8,128)S(1)}) custom-call(s32[256]{0:T(256)} %base_ids_h.1, s32[5]{0:T(128)} %comp_h.1, bf16[5,768]{1,0:T(8,128)(2,1)} %emb_h.1, bf16[768,768]{1,0:T(8,128)(2,1)} %w_gate_h.1, bf16[768,1024]{1,0:T(8,128)(2,1)} %w_mix_h.1, ...), custom_call_target="tpu_custom_call" | custom-call | tf_op jit(solution)/shard_map/tables/pallas_call | solution.py:350
  8.9 0.0 collective-permute-done
  9.0 0.1 collective-permute-start.1
  9.0 1.1 %collective-permute-done.1 = s32[2,256]{1,0:T(2,128)S(1)} collective-permute-done((s32[2,256]{1,0:T(2,128)S(1)}, s32[2,256]{1,0:T(2,128)S(1)}, u32[]{:S(2)}, u32[]{:S(2)}) %collective-permute-start.1) | collective-permute-done | bytes 2080 | tf_op jit(solution)/shard_map/ppermute | solution.py:372
  10.2 0.0 collective-permute-start.2
  10.2 2.8 %local.2 = (f32[2,256,768]{2,1,0:T(8,128)S(1)}, bf16[2,256,768]{2,1,0:T(8,128)(2,1)S(1)}, bf16[2,256,128]{2,1,0:T(8,128)(2,1)S(1)}) custom-call(s32[4,256]{1,0:T(4,128)S(1)} %add_select_fusion.3.window, bf16[2,64,2560]{2,1,0:T(8,128)(2,1)S(1)} %get-tuple-element.16.wide, f32[40,1024]{1,0:T(8,128)S(1)} %get-tuple-element.18.small), custom_call_target="tpu_custom_call" | custom-call | flops 4000000000 | tf_op jit(solution)/shard_map/local/pallas_call | solution.py:376
  13.0 0.2 %collective-permute-done.2 = s32[4,256]{1,0:T(4,128)S(1)} collective-permute-done((s32[4,256]{1,0:T(4,128)S(1)}, s32[4,256]{1,0:T(4,128)S(1)}, u32[]{:S(2)}, u32[]{:S(2)}) %collective-permute-start.2) | collective-permute-done | bytes 4128 | tf_op jit(solution)/shard_map/ppermute | solution.py:394
  13.2 1.0 %collective-permute-start.3 = (s32[8,256]{1,0:T(8,128)S(1)}, s32[8,256]{1,0:T(8,128)S(1)}, u32[]{:S(2)}, u32[]{:S(2)}) collective-permute-start(s32[8,256]{1,0:T(8,128)S(1)} %add_select_fusion.2.rest_0_), channel_id=1, source_target_pairs={{0,9},{1,8},{2,11},{3,10},{4,13},{5,12},{6,15},{7,14},{8,1},{9,0},... | collective-permute-start | bytes 24584 | tf_op jit(solution)/shard_map/ppermute | solution.py:394
  14.2 2.8 %local.3 = (f32[2,256,768]{2,1,0:T(8,128)S(1)}, bf16[2,256,768]{2,1,0:T(8,128)(2,1)S(1)}, bf16[2,256,128]{2,1,0:T(8,128)(2,1)S(1)}) custom-call(s32[4,256]{1,0:T(4,128)S(1)} %add_select_fusion.3.window, bf16[2,64,2560]{2,1,0:T(8,128)(2,1)S(1)} %get-tuple-element.16.wide, f32[40,1024]{1,0:T(8,128)S(1)} %get-tuple-element.18.small, ...), custom_call_target="tpu_custom_call" | custom-call | flops 4000000000 | tf_op jit(solution)/shard_map/local/pallas_call | solution.py:376
  17.0 0.2 collective-permute-done.3
  17.2 7.2 %finish.1 = bf16[256,768]{1,0:T(8,128)(2,1)} custom-call(s32[16,256]{1,0:T(8,128)S(1)} %add_select_fusion.1.ids, bf16[2,64,2560]{2,1,0:T(8,128)(2,1)S(1)} %get-tuple-element.16.wide, bf16[2,896,640]{2,1,0:T(8,128)(2,1)S(1)} %get-tuple-element.17.xt, f32[40,1024]{1,0:T(8,128)S(1)} %get-tuple-element.18.small, ...), custom_call_target="tpu_custom_call" | custom-call | tf_op jit(solution)/shard_map/finish/pallas_call | solution.py:404
  (7 shorter events, 0.1 us)
Async XLA Ops:
  0.0 8.9 %collective-permute-start = (s32[256]{0:T(256)}, s32[256]{0:T(256)S(1)}, u32[]{:S(2)}, u32[]{:S(2)}) collective-permute-start(s32[256]{0:T(256)} %base_ids_h.1), channel_id=1, source_target_pairs={{0,15},{1,2},{2,1},{3,4},{4,3},{5,6},{6,5},{7,8},{8,7},{9,10},{10,... | collective-permute-start | bytes 3080 | tf_op jit(solution)/shard_map/ppermute | solution.py:344
  9.0 1.2 %collective-permute-start.1 = (s32[2,256]{1,0:T(2,128)S(1)}, s32[2,256]{1,0:T(2,128)S(1)}, u32[]{:S(2)}, u32[]{:S(2)}) collective-permute-start(s32[2,256]{1,0:T(2,128)S(1)} %add_select_fusion.4), channel_id=1, source_target_pairs={{0,1},{1,0},{2,3},{3,2},{4,5},{5,4},{6,7},{7,6},{8,9},{9,8},{10,11... | collective-permute-start | bytes 6152 | tf_op jit(solution)/shard_map/ppermute | solution.py:372
  10.2 3.0 %collective-permute-start.2 = (s32[4,256]{1,0:T(4,128)S(1)}, s32[4,256]{1,0:T(4,128)S(1)}, u32[]{:S(2)}, u32[]{:S(2)}) collective-permute-start(s32[4,256]{1,0:T(4,128)S(1)} %add_select_fusion.3.window), channel_id=1, source_target_pairs={{0,5},{1,4},{2,7},{3,6},{4,1},{5,0},{6,3},{7,2},{8,13},{9,12},{10,... | collective-permute-start | bytes 12296 | tf_op jit(solution)/shard_map/ppermute | solution.py:394
  13.2 4.0 %collective-permute-start.3 = (s32[8,256]{1,0:T(8,128)S(1)}, s32[8,256]{1,0:T(8,128)S(1)}, u32[]{:S(2)}, u32[]{:S(2)}) collective-permute-start(s32[8,256]{1,0:T(8,128)S(1)} %add_select_fusion.2.rest_0_), channel_id=1, source_target_pairs={{0,9},{1,8},{2,11},{3,10},{4,13},{5,12},{6,15},{7,14},{8,1},{9,0},... | collective-permute-start | bytes 24584 | tf_op jit(solution)/shard_map/ppermute | solution.py:394

commit v3 on v2

--- a/solution.py
+++ b/solution.py
@@ -41,12 +41,16 @@
     return jnp.where(jnp.broadcast_to(row, (LETTER_ROWS, row.shape[1])) == iota((LETTER_ROWS, row.shape[1]), 0), 1.0, 0.0)
 
 
+def digits_of(before):
+    first = (before * 41) >> 10
+    pair = (before * 205) >> 10
+    return first, pair - 5 * first, before - 5 * pair
+
+
 def code_onehot(shape, code_dim):
     code, slot = iota(shape, code_dim), iota(shape, 1 - code_dim) & 31
     before, last = code & 127, code >> 7
-    first = (before * 41) >> 10
-    pair = (before * 205) >> 10
-    second, third = pair - 5 * first, before - 5 * pair
+    first, second, third = digits_of(before)
     tap = slot >> 3
     digit = jnp.where(tap == 0, first, jnp.where(tap == 1, second, jnp.where(tap == 2, third, last)))
     return jnp.where(digit == (slot & 7), 1.0, 0.0).astype(BF16)
@@ -60,15 +64,15 @@
 
 def tables_kernel(
     base_ids_h, comp_h, emb_h, w_gate_h, w_mix_h, w_step_h, step_bias_h, rate_h, conv_w_h, conv_b_h, skip_h,
-    norm_gain_h,
-    own, wide, xt, small,
+    norm_gain_h, w_out_h,
+    own, wide, xt, small, turn, w_out,
     e16, ids_v, comp, emb, w_gate, w_mix, w_step, step_bias, rate, conv_w, conv_b, skip, gain_v, sems,
     *, heads, head_dim, state,
 ):
     pairs = [
         (emb_h, emb), (comp_h, comp), (w_mix_h, w_mix), (w_step_h, w_step), (step_bias_h, step_bias), (rate_h, rate),
         (skip_h, skip), (conv_w_h, conv_w), (conv_b_h, conv_b), (w_gate_h, w_gate), (base_ids_h, ids_v),
-        (norm_gain_h, gain_v),
+        (norm_gain_h, gain_v), (w_out_h, w_out),
     ]
     copies = [pltpu.make_async_copy(a, b, sems.at[n]) for n, (a, b) in enumerate(pairs)]
     for copy in copies:
@@ -94,14 +98,14 @@
         small[strand * heads : (strand + 1) * heads, STEP_AT : STEP_AT + LETTER_ROWS] = step_t[:, at]
         for v in range(letters):
             small[strand * heads : (strand + 1) * heads, v * 128 : (v + 1) * 128] = jnp.broadcast_to(
-                step_t[:, strand * LETTER_ROWS + v : strand * LETTER_ROWS + v + 1], (heads, 128)
+                step_t[:, v : v + 1], (heads, 128)
             )
     spread = head_spread(heads, inner, head_dim).astype(BF16)
     steps = [dot(part.astype(BF16), spread) for part in split(step)]
     skip_high, skip_rest = split(skip[...].reshape(1, heads))
     skip_mid, skip_low = split(skip_rest)
     small[2 * heads : 2 * heads + 1, :inner] = sum(dot(part.astype(BF16), spread) for part in (skip_high, skip_mid, skip_low))
-    width, codes = conv_w.shape[1], xt.shape[2]
+    width, codes = conv_w.shape[1], xt.shape[1]
     by_column = code_onehot((64, codes), 1)
     for strand in range(2):
         letter_rows = mix[strand * LETTER_ROWS : (strand + 1) * LETTER_ROWS]
@@ -110,9 +114,17 @@
         high, low = split(jnp.concatenate(weighted, axis=0))
         both = jnp.concatenate([high, low], axis=0)
         wide[strand, :, :width] = both.astype(BF16)
-        across = jnp.transpose(both[:, : inner + state]).astype(BF16)
-        for low_row in range(0, inner + state, CHUNK):
-            xt[strand, low_row : low_row + CHUNK, :] = silu(dot(across[low_row : low_row + CHUNK], by_column)).astype(BF16)
+        if strand == 0:
+            across = jnp.transpose(both[:, : inner + state]).astype(BF16)
+            for low_row in range(0, inner + state, CHUNK):
+                part = silu(dot(across[low_row : low_row + CHUNK], by_column))
+                xt[low_row : low_row + CHUNK, :] = part.astype(BF16)
+    before = iota((128, 128), 0)
+    target = jnp.zeros((128, 128), I32)
+    for digit, worth in zip(digits_of(before), (25, 5, 1)):
+        for v in range(letters):
+            target = target + jnp.where(digit == v, comp[v] * worth, 0)
+    turn[...] = jnp.where((target == iota((128, 128), 1)) & (before < 125), 1.0, 0.0).astype(BF16)
     copies[9].wait()
     gate = silu(dot(rows, w_gate[...]).astype(BF16).astype(F32))
     gates = split(gate)
@@ -158,10 +170,11 @@
     full = sum(ld[:, v : v + 1] * count[v : v + 1, :] for v in range(5))
     less = sum(ld[:, v : v + 1] * before[v : v + 1, :] for v in range(5))
     full_t, less_t = jnp.transpose(full), jnp.transpose(less)
-    spread = head_spread(heads, inner, head_dim)
-    spread = spread.astype(BF16)
+    spread = head_spread(16, inner, head_dim)
+    spread = jnp.concatenate([spread, spread], axis=0).astype(BF16)
     enter = (jnp.exp(full), jnp.exp(full[:, length - 1 : length] - less))
-    enter = [[half.astype(BF16) for half in split(part)] for part in enter]
+    fill = jnp.zeros((4, length), F32)
+    enter = [jnp.concatenate([high, fill, low, fill], axis=0).astype(BF16) for high, low in map(split, enter)]
     row, lane = iota((CHUNK, CHUNK), 0), iota((CHUNK, CHUNK), 1)
     lower, upper = row >= lane, row <= lane
     first_half = iota((CHUNK, CHUNK), 1) < head_dim
@@ -178,17 +191,17 @@
         stepped.append((x * stepx).astype(BF16))
         scores.append(dot(read, keys, NT))
         eg[way] = (
-            sum(dot(half, spread, TN) for half in enter[way]) * gate
+            dot(enter[way], spread, TN) * gate
         ).astype(BF16)
     cut = {}
     for i in range(blocks):
         for j in range(blocks):
             if i >= j:
                 s = scores[0][span(i), span(j)]
-                cut[0, i, j] = jnp.where(lower, s, 0.0) if i == j else s
+                cut[0, i, j] = (jnp.where(lower, s, 0.0) if i == j else s).astype(BF16)
             if i <= j:
                 s = scores[1][span(i), span(j)]
-                cut[1, i, j] = jnp.where(upper, s, 0.0) if i == j else s
+                cut[1, i, j] = (jnp.where(upper, s, 0.0) if i == j else s).astype(BF16)
     for pair in range(heads // 2):
         columns = slice(pair * 2 * head_dim, (pair + 1) * 2 * head_dim)
         found = []
@@ -202,12 +215,12 @@
                     if i <= j:
                         up = less[k : k + 1, span(j)] - less_t[span(i), k : k + 1]
                     gap = down if i > j else up if i < j else jnp.where(lower, down, up)
-                    decay[i, j] = jnp.exp(gap)
+                    decay[i, j] = jnp.exp(gap.astype(BF16))
             for way in range(2):
                 out = []
                 for i in range(blocks):
                     js = range(i + 1) if way == 0 else range(i, blocks)
-                    weights = jnp.concatenate([(cut[way, i, j] * decay[i, j]).astype(BF16) for j in js], axis=1)
+                    weights = jnp.concatenate([cut[way, i, j] * decay[i, j] for j in js], axis=1)
                     out.append(dot(weights, stepped[way][js[0] * CHUNK : (js[-1] + 1) * CHUNK, columns]))
                 found.append(out)
         for way in range(2):
@@ -218,16 +231,16 @@
 
 
 def finish_kernel(
-    ids, wide, xt, small, reads0, yg0, eg0, reads1, yg1, eg1, w_out_h,
+    ids, wide, xt, small, turn, w_out, reads0, yg0, eg0, reads1, yg1, eg1, comp_h,
     out,
-    w_out, sem,
+    comp, moved, sem,
     *, heads, head_dim, state,
 ):
     members, length = ids.shape
     inner = heads * head_dim
     position = lax.axis_index("ctx")
     letters = 5
-    load = pltpu.make_async_copy(w_out_h, w_out, sem)
+    load = pltpu.make_async_copy(comp_h, comp, sem)
     load.start()
     every = ids[...]
     lane = iota((members, length), 1)
@@ -243,7 +256,9 @@
         after.append(jnp.where((block == members - 1) & (lane >= length - k), -1, found))
     code_ahead = jnp.where((block == 0) & (lane < 3), -1, prev[2] * 25 + prev[1] * 5 + prev[0])
     code_behind = jnp.where((block == members - 1) & (lane >= length - 3), -1, after[2] * 25 + after[1] * 5 + after[0])
-    code = jnp.where(block < position, code_ahead, code_behind)
+    code_behind = jnp.where(code_behind < 0, -1, code_behind + 128)
+    code = jnp.where(block < position, code_ahead, jnp.where(block > position, code_behind, -1)).astype(BF16)
+    code_rows = iota((256, length), 0).astype(BF16)
 
     marks = [onehot_rows(every[b : b + 1, :]) for b in range(members)]
     mark = jnp.concatenate(marks, axis=0)
@@ -270,19 +285,19 @@
         far_b = jnp.exp(sum(ld[:, v : v + 1] * count[v : v + 1, :] for v in range(letters)))
         if b in (0, members - 1):
             far[b] = far_b
-        by_last = [far_b * marks[b][v : v + 1, :] for v in range(letters)]
-        in_front = jnp.where(b < position, 1.0, 0.0)
-        in_back = jnp.where(b > position, 1.0, 0.0)
-        by_last = [part * in_front for part in by_last] + [part * in_back for part in by_last]
-        weighed.append(jnp.concatenate(by_last, axis=0).astype(BF16))
-        hot.append(jnp.where(iota((128, length), 0) == code[b : b + 1, :], 1.0, 0.0).astype(BF16))
+        weighed.append(jnp.concatenate([far_b * marks[b][v : v + 1, :] for v in range(letters)], axis=0).astype(BF16))
+        hot.append(jnp.where(code_rows == code[b : b + 1, :], BF16(1), BF16(0)))
     sums = dot(jnp.concatenate(weighed, axis=1), jnp.concatenate(hot, axis=1), NT)
 
     edge_lane = iota((1, 128), 1)
     tail = slice(length - 128, length)
     digits = [jnp.where(edge_lane < 64, prev[2 - k][0:1, :128], after[2 - k][members - 1 :, tail]) for k in range(3)]
     digits.append(jnp.where(edge_lane < 64, every[0:1, :128], every[members - 1 :, tail]))
-    edge_hot = jnp.concatenate([onehot_rows(d) for d in digits] * 2, axis=0).astype(BF16)
+    edge_hot = jnp.concatenate([onehot_rows(d) for d in digits] * 2, axis=0)
+    edge_hot = jnp.where((edge_lane < 3) | (edge_lane >= 125), edge_hot, 0.0)
+    edge_hot = jnp.concatenate([edge_hot, pltpu.roll(edge_hot, 8, 1)], axis=0).astype(BF16)
+    edge = silu(dot(wide[:, :, : inner + state].reshape(128, inner + state), edge_hot, TN)).astype(BF16)
+    keys = jnp.concatenate([xt[inner:, :], edge[inner:]], axis=1)
     st = small[: 2 * heads, STEP_AT : STEP_AT + LETTER_ROWS]
     stepk = small[: 2 * heads, : letters * 128]
     first_step = sum(st[:, v : v + 1] * marks[0][v : v + 1, :128] for v in range(letters))
@@ -294,26 +309,32 @@
     span = 2 * heads
     total = jnp.zeros((length, inner), F32)
     weights = []
-    for way, edge in enumerate((edge_ahead, edge_behind)):
+    load.wait()
+    first_strand = iota((span, 1), 0) < heads
+    both = jnp.concatenate([sums[:, :128], sums[:, 128:]], axis=0)
+    turned = dot(both.astype(BF16), turn[...])
+    for way, rim in enumerate((edge_ahead, edge_behind)):
         base = way * letters * span
-        by_code = jnp.concatenate([sums[base + v * span : base + (v + 1) * span] for v in range(letters)], axis=1)
-        weights.append(jnp.concatenate([by_code * stepk, edge], axis=1).astype(BF16))
+        by_code = jnp.concatenate([both[base + v * span : base + (v + 1) * span] for v in range(letters)], axis=1)
+        for v in range(letters):
+            at = pl.multiple_of(comp[v] * 128, 128)
+            moved[way, :, pl.ds(at, 128)] = turned[base + v * span : base + (v + 1) * span]
+        by_code = jnp.where(first_strand, by_code, moved[way]) * stepk
+        rim = jnp.where(first_strand, rim, pltpu.roll(rim, 8, 1))
+        weights.append(jnp.concatenate([by_code, rim], axis=1).astype(BF16))
     for strand in range(2):
-        edge = silu(dot(wide[strand, :, : inner + state], edge_hot, TN)).astype(BF16)
-        keys = jnp.concatenate([xt[strand, inner:, :], edge[inner:]], axis=1)
         for way in range(2):
             scaled = []
             for head in range(heads):
                 at = slice(head * head_dim, (head + 1) * head_dim)
-                x_head = jnp.concatenate([xt[strand, at, :], edge[at]], axis=1)
+                x_head = jnp.concatenate([xt[at, :], edge[at]], axis=1)
                 scaled.append(x_head * weights[way][strand * heads + head : strand * heads + head + 1, :])
-            entering = dot(jnp.concatenate(scaled, axis=0), keys, NT).astype(BF16)
+            entering = dot(keys, jnp.concatenate(scaled, axis=0), NT).astype(BF16)
             reads, yg, eg = ((reads0, yg0, eg0), (reads1, yg1, eg1))[strand]
-            carried = dot(reads[way], entering, NT)
+            carried = dot(reads[way], entering)
             g = yg[way] + carried * eg[way].astype(F32)
             power = jnp.sum(g * g, axis=1, keepdims=True) * (1.0 / inner)
             total = total + g * lax.rsqrt(power + 1e-05)
-    load.wait()
     out[...] = dot((total * small[GAIN_AT : GAIN_AT + 1, :inner]).astype(BF16), w_out[...]).astype(BF16)
 
 
@@ -345,18 +366,20 @@
 
     given = (
         base_ids, complement, embedding, w_gate, w_mix, w_step.T, step_bias, decay_rate, conv_weight, conv_bias,
-        skip_gain, norm_gain,
+        skip_gain, norm_gain, w_out,
     )
-    own, wide, xt, small = pl.pallas_call(
+    own, wide, xt, small, turn, w_out_v = pl.pallas_call(
         functools.partial(tables_kernel, **sizes),
         out_shape=[
             shape((1, length), I32),
             shape((2, 64, width + 2 * inner), BF16),
-            shape((2, inner + state, codes), BF16),
+            shape((inner + state, codes), BF16),
             shape((40, 1024), F32),
+            shape((128, 128), BF16),
+            shape(w_out.shape, BF16),
         ],
         in_specs=[hbm] * len(given),
-        out_specs=[vmem] * 4,
+        out_specs=[vmem] * 6,
         scratch_shapes=[
             VMEM((2 * LETTER_ROWS, depth), F32),
             VMEM(base_ids.shape, I32),
@@ -404,12 +427,19 @@
     return pl.pallas_call(
         functools.partial(finish_kernel, **sizes),
         out_shape=jax.ShapeDtypeStruct((length, w_out.shape[1]), BF16),
-        in_specs=[vmem] * 10 + [hbm],
+        in_specs=[vmem] * 12 + [hbm],
         out_specs=vmem,
-        scratch_shapes=[VMEM(w_out.shape, BF16), pltpu.SemaphoreType.DMA(())],
+        scratch_shapes=[
+            pltpu.SMEM(complement.shape, I32),
+            VMEM((2, 2 * heads, codes), F32),
+            pltpu.SemaphoreType.DMA(()),
+        ],
         compiler_params=params,
         name="finish",
-    )(*[held(a) for a in (ids, wide, xt, small, reads0, yg0, eg0, reads1, yg1, eg1)], outside(w_out))
+    )(
+        *[held(a) for a in (ids, wide, xt, small, turn, w_out_v, reads0, yg0, eg0, reads1, yg1, eg1)],
+        outside(complement),
+    )
 
 
 def solution(mesh):

time: 24.7 us -> 22.8 us (0.923)
  Pallas kernels: 16.2 us -> 13.4 us
  waiting for transfers between devices: 1.57 us -> 3.01 us
  starting transfers between devices: 6.51 us -> 6.03 us
    ppermute x2, waiting for transfers between devices: 0.43 us -> 1.87 us  [on_device(): got = lax.ppermute(ids, 'ctx', [(i, i ^ bit ^ 1) for i in range(members)])]
    pallas_call x1, Pallas kernels: 7.2 us -> 5.76 us  [on_device(): pl.pallas_call(functools.partial(finish_kernel, **sizes), out_shape=jax.S...]
    pallas_call x2, Pallas kernels: 5.54 us -> 4.57 us  [local(): pl.pallas_call(functools.partial(local_kernel, strand=strand, **sizes), o...]
    ppermute x2, starting transfers between devices: 1.02 us -> 0.54 us  [on_device(): got = lax.ppermute(ids, 'ctx', [(i, i ^ bit ^ 1) for i in range(members)])]
    pallas_call x1, Pallas kernels: 3.5 us -> 3.08 us  [on_device(): pl.pallas_call(functools.partial(tables_kernel, **sizes), out_shape=[shap...]
  transfers between devices with their start and end apart: 4 -> 4, of which waited for: 3 -> 3; matrix products, arithmetic and copies ran while one was open for 0% -> 0% of each run, Pallas kernels for 37% -> 34%
where the time goes in v3:
time: 22.8 us; the launch traced here: 22.6 us
  Pallas kernels  13.4 us (59%)
  starting transfers between devices  6.03 us (26%)
  waiting for transfers between devices  3.01 us (13%)
    pallas_call x1, Pallas kernels, on_device(): pl.pallas_call(functools.partial(finish_kernel, **sizes), out_shape=jax.S...  5.76 us
    ppermute x1, starting transfers between devices, on_device(): other = lax.ppermute(base_ids, 'ctx', across).reshape(1, length)  5.42 us
    pallas_call x2, Pallas kernels, local(): pl.pallas_call(functools.partial(local_kernel, strand=strand, **sizes), o...  4.57 us
    pallas_call x1, Pallas kernels, on_device(): pl.pallas_call(functools.partial(tables_kernel, **sizes), out_shape=[shap...  3.08 us
    ppermute x2, waiting for transfers between devices, on_device(): got = lax.ppermute(ids, 'ctx', [(i, i ^ bit ^ 1) for i in range(members)])  1.87 us
    ppermute x1, waiting for transfers between devices, on_device(): got = lax.ppermute(two, 'ctx', [(i, i ^ 1) for i in range(members)])  1.13 us
    ppermute x2, starting transfers between devices, on_device(): got = lax.ppermute(ids, 'ctx', [(i, i ^ bit ^ 1) for i in range(members)])  0.54 us
  transfers between devices with their start and end apart: 4, of which 3 were waited for; matrix products, arithmetic and copies ran while one was open for 0% of the time, Pallas kernels for 34%

profile of v3, /device:TPU:0, one launch (start us, length us, event | category | flops | bytes accessed | tf_op | source)
XLA Modules:
  0.0 22.6 jit_solution(11838503907073762825)
XLA Ops:
  0.0 5.4 %collective-permute-start = (s32[256]{0:T(256)}, s32[256]{0:T(256)S(1)}, u32[]{:S(2)}, u32[]{:S(2)}) collective-permute-start(s32[256]{0:T(256)} %base_ids_h.1), channel_id=1, source_target_pairs={{0,15},{1,2},{2,1},{3,4},{4,3},{5,6},{6,5},{7,8},{8,7},{9,10},{10,... | collective-permute-start | bytes 3080 | tf_op jit(solution)/shard_map/ppermute | solution.py:365
  5.4 3.1 %tables.1 = (s32[1,256]{1,0:T(1,128)S(1)}, bf16[2,64,2560]{2,1,0:T(8,128)(2,1)S(1)}, bf16[896,640]{1,0:T(8,128)(2,1)S(1)}, f32[40,1024]{1,0:T(8,128)S(1)}, bf16[...) custom-call(s32[256]{0:T(256)} %base_ids_h.1, s32[5]{0:T(128)} %comp_h.3, bf16[5,768]{1,0:T(8,128)(2,1)} %emb_h.1, ...), custom_call_target="tpu_custom_call" | custom-call | tf_op jit(solution)/shard_map/tables/pallas_call | solution.py:371
  8.5 0.0 collective-permute-done
  8.5 0.1 collective-permute-start.1
  8.6 1.1 %collective-permute-done.1 = s32[2,256]{1,0:T(2,128)S(1)} collective-permute-done((s32[2,256]{1,0:T(2,128)S(1)}, s32[2,256]{1,0:T(2,128)S(1)}, u32[]{:S(2)}, u32[]{:S(2)}) %collective-permute-start.1) | collective-permute-done | bytes 2080 | tf_op jit(solution)/shard_map/ppermute | solution.py:395
  9.8 0.0 collective-permute-start.2
  9.8 2.3 %local.2 = (f32[2,256,768]{2,1,0:T(8,128)S(1)}, bf16[2,256,768]{2,1,0:T(8,128)(2,1)S(1)}, bf16[2,256,128]{2,1,0:T(8,128)(2,1)S(1)}) custom-call(s32[4,256]{1,0:T(4,128)S(1)} %add_select_fusion.3.window, bf16[2,64,2560]{2,1,0:T(8,128)(2,1)S(1)} %get-tuple-element.18.wide, f32[40,1024]{1,0:T(8,128)S(1)} %get-tuple-element.20.small), custom_call_target="tpu_custom_call" | custom-call | flops 4000000000 | tf_op jit(solution)/shard_map/local/pallas_call | solution.py:399
  12.1 0.7 %collective-permute-done.2 = s32[4,256]{1,0:T(4,128)S(1)} collective-permute-done((s32[4,256]{1,0:T(4,128)S(1)}, s32[4,256]{1,0:T(4,128)S(1)}, u32[]{:S(2)}, u32[]{:S(2)}) %collective-permute-start.2) | collective-permute-done | bytes 4128 | tf_op jit(solution)/shard_map/ppermute | solution.py:417
  12.8 0.5 %collective-permute-start.3 = (s32[8,256]{1,0:T(8,128)S(1)}, s32[8,256]{1,0:T(8,128)S(1)}, u32[]{:S(2)}, u32[]{:S(2)}) collective-permute-start(s32[8,256]{1,0:T(8,128)S(1)} %add_select_fusion.2.rest_0_), channel_id=1, source_target_pairs={{0,9},{1,8},{2,11},{3,10},{4,13},{5,12},{6,15},{7,14},{8,1},{9,0},... | collective-permute-start | bytes 24584 | tf_op jit(solution)/shard_map/ppermute | solution.py:417
  13.3 2.3 %local.3 = (f32[2,256,768]{2,1,0:T(8,128)S(1)}, bf16[2,256,768]{2,1,0:T(8,128)(2,1)S(1)}, bf16[2,256,128]{2,1,0:T(8,128)(2,1)S(1)}) custom-call(s32[4,256]{1,0:T(4,128)S(1)} %add_select_fusion.3.window, bf16[2,64,2560]{2,1,0:T(8,128)(2,1)S(1)} %get-tuple-element.18.wide, f32[40,1024]{1,0:T(8,128)S(1)} %get-tuple-element.20.small, ...), custom_call_target="tpu_custom_call" | custom-call | flops 4000000000 | tf_op jit(solution)/shard_map/local/pallas_call | solution.py:399
  15.6 1.1 %collective-permute-done.3 = s32[8,256]{1,0:T(8,128)S(1)} collective-permute-done((s32[8,256]{1,0:T(8,128)S(1)}, s32[8,256]{1,0:T(8,128)S(1)}, u32[]{:S(2)}, u32[]{:S(2)}) %collective-permute-start.3) | collective-permute-done | bytes 8224 | tf_op jit(solution)/shard_map/ppermute | solution.py:417
  16.8 5.8 %finish.1 = bf16[256,768]{1,0:T(8,128)(2,1)} custom-call(s32[16,256]{1,0:T(8,128)S(1)} %add_select_fusion.1.ids, bf16[2,64,2560]{2,1,0:T(8,128)(2,1)S(1)} %get-tuple-element.18.wide, bf16[896,640]{1,0:T(8,128)(2,1)S(1)} %get-tuple-element.19.xt, f32[40,1024]{1,0:T(8,128)S(1)} %get-tuple-element.20.small, bf16[128,128]{1,0:T(8,128)(2,1)S(1)} %get-tuple-element.21.turn, ...), custom_call_target="tpu_custom_call" | custom-call | tf_op jit(solution)/shard_map/finish/pallas_call | solution.py:427
  (7 shorter events, 0.1 us)
Async XLA Ops:
  0.0 8.5 %collective-permute-start = (s32[256]{0:T(256)}, s32[256]{0:T(256)S(1)}, u32[]{:S(2)}, u32[]{:S(2)}) collective-permute-start(s32[256]{0:T(256)} %base_ids_h.1), channel_id=1, source_target_pairs={{0,15},{1,2},{2,1},{3,4},{4,3},{5,6},{6,5},{7,8},{8,7},{9,10},{10,... | collective-permute-start | bytes 3080 | tf_op jit(solution)/shard_map/ppermute | solution.py:365
  8.5 1.2 %collective-permute-start.1 = (s32[2,256]{1,0:T(2,128)S(1)}, s32[2,256]{1,0:T(2,128)S(1)}, u32[]{:S(2)}, u32[]{:S(2)}) collective-permute-start(s32[2,256]{1,0:T(2,128)S(1)} %add_select_fusion.4), channel_id=1, source_target_pairs={{0,1},{1,0},{2,3},{3,2},{4,5},{5,4},{6,7},{7,6},{8,9},{9,8},{10,11... | collective-permute-start | bytes 6152 | tf_op jit(solution)/shard_map/ppermute | solution.py:395
  9.8 3.0 %collective-permute-start.2 = (s32[4,256]{1,0:T(4,128)S(1)}, s32[4,256]{1,0:T(4,128)S(1)}, u32[]{:S(2)}, u32[]{:S(2)}) collective-permute-start(s32[4,256]{1,0:T(4,128)S(1)} %add_select_fusion.3.window), channel_id=1, source_target_pairs={{0,5},{1,4},{2,7},{3,6},{4,1},{5,0},{6,3},{7,2},{8,13},{9,12},{10,... | collective-permute-start | bytes 12296 | tf_op jit(solution)/shard_map/ppermute | solution.py:417
  12.8 4.0 %collective-permute-start.3 = (s32[8,256]{1,0:T(8,128)S(1)}, s32[8,256]{1,0:T(8,128)S(1)}, u32[]{:S(2)}, u32[]{:S(2)}) collective-permute-start(s32[8,256]{1,0:T(8,128)S(1)} %add_select_fusion.2.rest_0_), channel_id=1, source_target_pairs={{0,9},{1,8},{2,11},{3,10},{4,13},{5,12},{6,15},{7,14},{8,1},{9,0},... | collective-permute-start | bytes 24584 | tf_op jit(solution)/shard_map/ppermute | solution.py:417

commit v4 on v3

--- a/solution.py
+++ b/solution.py
@@ -64,15 +64,15 @@
 
 def tables_kernel(
     base_ids_h, comp_h, emb_h, w_gate_h, w_mix_h, w_step_h, step_bias_h, rate_h, conv_w_h, conv_b_h, skip_h,
-    norm_gain_h, w_out_h,
-    own, wide, xt, small, turn, w_out,
+    norm_gain_h,
+    own, wide, small,
     e16, ids_v, comp, emb, w_gate, w_mix, w_step, step_bias, rate, conv_w, conv_b, skip, gain_v, sems,
     *, heads, head_dim, state,
 ):
     pairs = [
         (emb_h, emb), (comp_h, comp), (w_mix_h, w_mix), (w_step_h, w_step), (step_bias_h, step_bias), (rate_h, rate),
         (skip_h, skip), (conv_w_h, conv_w), (conv_b_h, conv_b), (w_gate_h, w_gate), (base_ids_h, ids_v),
-        (norm_gain_h, gain_v), (w_out_h, w_out),
+        (norm_gain_h, gain_v),
     ]
     copies = [pltpu.make_async_copy(a, b, sems.at[n]) for n, (a, b) in enumerate(pairs)]
     for copy in copies:
@@ -105,8 +105,7 @@
     skip_high, skip_rest = split(skip[...].reshape(1, heads))
     skip_mid, skip_low = split(skip_rest)
     small[2 * heads : 2 * heads + 1, :inner] = sum(dot(part.astype(BF16), spread) for part in (skip_high, skip_mid, skip_low))
-    width, codes = conv_w.shape[1], xt.shape[1]
-    by_column = code_onehot((64, codes), 1)
+    width = conv_w.shape[1]
     for strand in range(2):
         letter_rows = mix[strand * LETTER_ROWS : (strand + 1) * LETTER_ROWS]
         weighted = [conv_w[k : k + 1, :] * letter_rows for k in range(4)]
@@ -114,17 +113,6 @@
         high, low = split(jnp.concatenate(weighted, axis=0))
         both = jnp.concatenate([high, low], axis=0)
         wide[strand, :, :width] = both.astype(BF16)
-        if strand == 0:
-            across = jnp.transpose(both[:, : inner + state]).astype(BF16)
-            for low_row in range(0, inner + state, CHUNK):
-                part = silu(dot(across[low_row : low_row + CHUNK], by_column))
-                xt[low_row : low_row + CHUNK, :] = part.astype(BF16)
-    before = iota((128, 128), 0)
-    target = jnp.zeros((128, 128), I32)
-    for digit, worth in zip(digits_of(before), (25, 5, 1)):
-        for v in range(letters):
-            target = target + jnp.where(digit == v, comp[v] * worth, 0)
-    turn[...] = jnp.where((target == iota((128, 128), 1)) & (before < 125), 1.0, 0.0).astype(BF16)
     copies[9].wait()
     gate = silu(dot(rows, w_gate[...]).astype(BF16).astype(F32))
     gates = split(gate)
@@ -139,11 +127,95 @@
     small[GAIN_AT : GAIN_AT + 1, :inner] = gain_v[...].reshape(1, inner)
 
 
+def codes_kernel(
+    wide, _, comp_h, w_out_h,
+    xt, turn, w_out,
+    comp, sems,
+):
+    load, load_out = pltpu.make_async_copy(comp_h, comp, sems.at[0]), pltpu.make_async_copy(w_out_h, w_out, sems.at[1])
+    load.start()
+    load_out.start()
+    by_column = code_onehot((64, xt.shape[1]), 1)
+    across = jnp.transpose(wide[0, :, : xt.shape[0]].astype(F32)).astype(BF16)
+    for low_row in range(0, xt.shape[0], CHUNK):
+        part = silu(dot(across[low_row : low_row + CHUNK], by_column))
+        xt[low_row : low_row + CHUNK, :] = part.astype(BF16)
+    load.wait()
+    before = iota((128, 128), 0)
+    target = jnp.zeros((128, 128), I32)
+    for digit, worth in zip(digits_of(before), (25, 5, 1)):
+        for v in range(comp.shape[0]):
+            target = target + jnp.where(digit == v, comp[v] * worth, 0)
+    turn[...] = jnp.where((target == iota((128, 128), 1)) & (before < 125), 1.0, 0.0).astype(BF16)
+    load_out.wait()
+
+
+def survey(every, start, members, position):
+    rows, length = every.shape
+    lane = iota((rows, length), 1)
+    block = (iota((rows, length), 0) + start) & (members - 1)
+    prev, after = [], []
+    up, down = pltpu.roll(every, 1, 0), pltpu.roll(every, rows - 1, 0)
+    for k in (1, 2, 3):
+        inside, outside = pltpu.roll(every, k, 1), pltpu.roll(up, k, 1)
+        found = jnp.where(lane >= k, inside, outside)
+        prev.append(jnp.where((block == 0) & (lane < k), -1, found))
+        inside, outside = pltpu.roll(every, length - k, 1), pltpu.roll(down, length - k, 1)
+        found = jnp.where(lane < length - k, inside, outside)
+        after.append(jnp.where((block == members - 1) & (lane >= length - k), -1, found))
+    code_ahead = jnp.where((block == 0) & (lane < 3), -1, prev[2] * 25 + prev[1] * 5 + prev[0])
+    code_behind = after[2] * 25 + after[1] * 5 + after[0] + 128
+    code_behind = jnp.where((block == members - 1) & (lane >= length - 3), -1, code_behind)
+    code = jnp.where(block < position, code_ahead, jnp.where(block > position, code_behind, -1)).astype(BF16)
+
+    mark = jnp.concatenate([onehot_rows(every[b : b + 1, :]) for b in range(rows)], axis=0)
+    groups = rows * LETTER_ROWS
+    its_block = ((iota((groups, 1), 0) >> 3) + start) & (members - 1)
+    i, j = iota((groups, groups), 0), iota((groups, groups), 1)
+    bi, bj = ((i >> 3) + start) & (members - 1), ((j >> 3) + start) & (members - 1)
+    between = ((bi < bj) & (bj < position)) | ((position < bj) & (bj < bi))
+    between = jnp.where(((i & 7) == (j & 7)) & between, 1.0, 0.0).astype(BF16)
+    amid = dot(between, mark.astype(BF16)).astype(BF16)
+    s, t = iota((length, length), 0), iota((length, length), 1)
+    later = jnp.where(s > t, 1.0, 0.0).astype(BF16)
+    earlier = jnp.where(s < t, 1.0, 0.0).astype(BF16)
+    ones = jnp.ones((length, length), BF16)
+    counts = (
+        dot(jnp.where(its_block < position, mark, 0.0).astype(BF16), later)
+        + dot(jnp.where(its_block > position, mark, 0.0).astype(BF16), earlier)
+        + dot(amid, ones)
+    )
+    return code, mark, counts, prev, after
+
+
+def decayed(ld, count):
+    return jnp.exp(sum(ld[:, v : v + 1] * count[v : v + 1, :] for v in range(5)))
+
+
+def code_sums(code, mark, counts, ld):
+    rows, length = code.shape
+    code_rows = iota((256, length), 0).astype(BF16)
+    weighed, hot = [], []
+    for b in range(rows):
+        at = slice(b * LETTER_ROWS, (b + 1) * LETTER_ROWS)
+        far = decayed(ld, counts[at])
+        weighed.append(jnp.concatenate([far * mark[at][v : v + 1, :] for v in range(5)], axis=0).astype(BF16))
+        hot.append(jnp.where(code_rows == code[b : b + 1, :], BF16(1), BF16(0)))
+    return dot(jnp.concatenate(weighed, axis=1), jnp.concatenate(hot, axis=1), NT)
+
+
+def ring_start(position):
+    return jnp.where((position & 2) == 0, -1, 1)
+
+
 def local_kernel(
     window, wide, small, *rest,
     strand, heads, head_dim, state,
 ):
-    yg, eg, reads = rest[-3:]
+    if len(rest) == 5:
+        near_ids, yg, eg, reads, near = rest
+    else:
+        yg, eg, reads = rest
     length, inner = window.shape[1], heads * head_dim
     blocks = length // CHUNK
     members, position = lax.axis_size("ctx"), lax.axis_index("ctx")
@@ -228,13 +300,20 @@
                 y = jnp.where(first_half, found[way][i], found[2 + way][i])
                 y = y + skipx[:, columns] * values[way][span(i), columns]
                 yg[way, span(i), columns] = y * gate[span(i), columns]
+    if len(rest) == 5:
+        rows = near_ids.shape[0]
+        start = (position & (members - rows)) + ring_start(position)
+        code, mark, counts, _, _ = survey(near_ids[...], start, members, position)
+        inner_rows = slice(LETTER_ROWS, (rows - 1) * LETTER_ROWS)
+        every_ld = small[: 2 * heads, DECAY_AT : DECAY_AT + LETTER_ROWS]
+        near[...] = code_sums(code[1 : rows - 1], mark[inner_rows], counts[inner_rows], every_ld)
 
 
 def finish_kernel(
-    ids, wide, xt, small, turn, w_out, reads0, yg0, eg0, reads1, yg1, eg1, comp_h,
+    ids, wide, xt, small, turn, w_out, reads0, yg0, eg0, reads1, yg1, eg1, near, comp_h,
     out,
     comp, moved, sem,
-    *, heads, head_dim, state,
+    *, heads, head_dim, state, near_rows,
 ):
     members, length = ids.shape
     inner = heads * head_dim
@@ -243,56 +322,37 @@
     load = pltpu.make_async_copy(comp_h, comp, sem)
     load.start()
     every = ids[...]
-    lane = iota((members, length), 1)
-    block = iota((members, length), 0)
-    prev, after = [], []
-    up, down = pltpu.roll(every, 1, 0), pltpu.roll(every, members - 1, 0)
-    for k in (1, 2, 3):
-        inside, outside = pltpu.roll(every, k, 1), pltpu.roll(up, k, 1)
-        found = jnp.where(lane >= k, inside, outside)
-        prev.append(jnp.where((block == 0) & (lane < k), -1, found))
-        inside, outside = pltpu.roll(every, length - k, 1), pltpu.roll(down, length - k, 1)
-        found = jnp.where(lane < length - k, inside, outside)
-        after.append(jnp.where((block == members - 1) & (lane >= length - k), -1, found))
-    code_ahead = jnp.where((block == 0) & (lane < 3), -1, prev[2] * 25 + prev[1] * 5 + prev[0])
-    code_behind = jnp.where((block == members - 1) & (lane >= length - 3), -1, after[2] * 25 + after[1] * 5 + after[0])
-    code_behind = jnp.where(code_behind < 0, -1, code_behind + 128)
-    code = jnp.where(block < position, code_ahead, jnp.where(block > position, code_behind, -1)).astype(BF16)
-    code_rows = iota((256, length), 0).astype(BF16)
-
-    marks = [onehot_rows(every[b : b + 1, :]) for b in range(members)]
-    mark = jnp.concatenate(marks, axis=0)
-    rows = members * LETTER_ROWS
-    its_block = iota((rows, 1), 0) >> 3
-    i, j = iota((rows, rows), 0), iota((rows, rows), 1)
-    bi, bj = i >> 3, j >> 3
-    between = ((bi < bj) & (bj < position)) | ((position < bj) & (bj < bi))
-    between = jnp.where(((i & 7) == (j & 7)) & between, 1.0, 0.0).astype(BF16)
-    amid = dot(between, mark.astype(BF16)).astype(BF16)
-    s, t = iota((length, length), 0), iota((length, length), 1)
-    later = jnp.where(s > t, 1.0, 0.0).astype(BF16)
-    earlier = jnp.where(s < t, 1.0, 0.0).astype(BF16)
-    ones = jnp.ones((length, length), BF16)
-    counts = (
-        dot(jnp.where(its_block < position, mark, 0.0).astype(BF16), later)
-        + dot(jnp.where(its_block > position, mark, 0.0).astype(BF16), earlier)
-        + dot(amid, ones)
-    )
+    start = ring_start(position)
+    code, mark, counts, prev, after = survey(every, start, members, position)
     ld = small[: 2 * heads, DECAY_AT : DECAY_AT + LETTER_ROWS]
-    weighed, hot, far = [], [], {}
-    for b in range(members):
-        count = counts[b * LETTER_ROWS : (b + 1) * LETTER_ROWS]
-        far_b = jnp.exp(sum(ld[:, v : v + 1] * count[v : v + 1, :] for v in range(letters)))
-        if b in (0, members - 1):
-            far[b] = far_b
-        weighed.append(jnp.concatenate([far_b * marks[b][v : v + 1, :] for v in range(letters)], axis=0).astype(BF16))
-        hot.append(jnp.where(code_rows == code[b : b + 1, :], BF16(1), BF16(0)))
-    sums = dot(jnp.concatenate(weighed, axis=1), jnp.concatenate(hot, axis=1), NT)
+    low = position & (members - near_rows)
+    if members == 2 * near_rows:
+
+        def rest(value, size):
+            part = lambda a, b: value[a * size : b * size]
+            n, m = near_rows, members
+            below = jnp.concatenate([part(0, 1), part(n - 1, n), part(n, m)], axis=0)
+            above = jnp.concatenate([part(n, n + 1), part(m - 1, m), part(0, n)], axis=0)
+            return jnp.where(low == 0, below, above)
+
+        sums = code_sums(rest(code.astype(F32), 1).astype(BF16), rest(mark, LETTER_ROWS), rest(counts, LETTER_ROWS), ld)
+    else:
+        row = iota((members, length), 0)
+        code = jnp.where((row > low) & (row < low + near_rows - 1), -1.0, code.astype(F32)).astype(BF16)
+        sums = code_sums(code, mark, counts, ld)
+    sums = sums + near[...]
+    even = start < 0
+
+    def end_rows(value, size, last):
+        at = (0, members - 2) if last else (1, members - 1)
+        return jnp.where(even, *[value[n * size : (n + 1) * size] for n in at])
 
     edge_lane = iota((1, 128), 1)
     tail = slice(length - 128, length)
-    digits = [jnp.where(edge_lane < 64, prev[2 - k][0:1, :128], after[2 - k][members - 1 :, tail]) for k in range(3)]
-    digits.append(jnp.where(edge_lane < 64, every[0:1, :128], every[members - 1 :, tail]))
+    digits = [
+        jnp.where(edge_lane < 64, end_rows(before, 1, False)[:, :128], end_rows(behind, 1, True)[:, tail])
+        for before, behind in zip(prev[::-1] + [every], after[::-1] + [every])
+    ]
     edge_hot = jnp.concatenate([onehot_rows(d) for d in digits] * 2, axis=0)
     edge_hot = jnp.where((edge_lane < 3) | (edge_lane >= 125), edge_hot, 0.0)
     edge_hot = jnp.concatenate([edge_hot, pltpu.roll(edge_hot, 8, 1)], axis=0).astype(BF16)
@@ -300,12 +360,13 @@
     keys = jnp.concatenate([xt[inner:, :], edge[inner:]], axis=1)
     st = small[: 2 * heads, STEP_AT : STEP_AT + LETTER_ROWS]
     stepk = small[: 2 * heads, : letters * 128]
-    first_step = sum(st[:, v : v + 1] * marks[0][v : v + 1, :128] for v in range(letters))
-    last_step = sum(st[:, v : v + 1] * marks[members - 1][v : v + 1, tail] for v in range(letters))
-    edge_ahead = jnp.where((edge_lane < 3) & (position > 0), far[0][:, :128] * first_step, 0.0)
-    edge_behind = jnp.where(
-        (edge_lane >= 125) & (position < members - 1), far[members - 1][:, tail] * last_step, 0.0
-    )
+    ends = []
+    for last, lanes in ((False, slice(0, 128)), (True, tail)):
+        marks = end_rows(mark, LETTER_ROWS, last)[:, lanes]
+        step = sum(st[:, v : v + 1] * marks[v : v + 1, :] for v in range(letters))
+        ends.append(decayed(ld, end_rows(counts, LETTER_ROWS, last)[:, lanes]) * step)
+    edge_ahead = jnp.where((edge_lane < 3) & (position > 0), ends[0], 0.0)
+    edge_behind = jnp.where((edge_lane >= 125) & (position < members - 1), ends[1], 0.0)
     span = 2 * heads
     total = jnp.zeros((length, inner), F32)
     weights = []
@@ -366,20 +427,17 @@
 
     given = (
         base_ids, complement, embedding, w_gate, w_mix, w_step.T, step_bias, decay_rate, conv_weight, conv_bias,
-        skip_gain, norm_gain, w_out,
+        skip_gain, norm_gain,
     )
-    own, wide, xt, small, turn, w_out_v = pl.pallas_call(
+    own, wide, small = pl.pallas_call(
         functools.partial(tables_kernel, **sizes),
         out_shape=[
             shape((1, length), I32),
             shape((2, 64, width + 2 * inner), BF16),
-            shape((inner + state, codes), BF16),
             shape((40, 1024), F32),
-            shape((128, 128), BF16),
-            shape(w_out.shape, BF16),
         ],
         in_specs=[hbm] * len(given),
-        out_specs=[vmem] * 6,
+        out_specs=[vmem] * 3,
         scratch_shapes=[
             VMEM((2 * LETTER_ROWS, depth), F32),
             VMEM(base_ids.shape, I32),
@@ -393,18 +451,30 @@
 
     two = jnp.where(odd, jnp.concatenate([own, other]), jnp.concatenate([other, own]))
     got = lax.ppermute(two, "ctx", [(i, i ^ 1) for i in range(members)])
+    xt, turn, w_out_v = pl.pallas_call(
+        codes_kernel,
+        out_shape=[shape((inner + state, codes), BF16), shape((128, 128), BF16), shape(w_out.shape, BF16)],
+        in_specs=[vmem] * 2 + [hbm] * 2,
+        out_specs=[vmem] * 3,
+        scratch_shapes=[pltpu.SMEM(complement.shape, I32), pltpu.SemaphoreType.DMA((2,))],
+        compiler_params=params,
+        cost_estimate=pl.CostEstimate(flops=2_000_000_000, bytes_accessed=0, transcendentals=0),
+        name="codes",
+    )(held(wide), held(two), outside(complement), outside(w_out))
     window = jnp.where(odd, jnp.concatenate([got, two]), jnp.concatenate([two, got]))
 
     def local(strand, *after):
+        near = [shape((5 * 2 * heads, 256), F32)] * len(after)
         return pl.pallas_call(
             functools.partial(local_kernel, strand=strand, **sizes),
             out_shape=[
                 shape((2, length, inner), F32),
                 shape((2, length, inner), BF16),
                 shape((2, length, state), BF16),
-            ],
+            ]
+            + near,
             in_specs=[vmem] * (3 + len(after)),
-            out_specs=[vmem] * 3,
+            out_specs=[vmem] * (3 + len(after)),
             compiler_params=params,
             cost_estimate=pl.CostEstimate(flops=4_000_000_000, bytes_accessed=0, transcendentals=0),
             name="local",
@@ -416,18 +486,15 @@
     while bit < members:
         got = lax.ppermute(ids, "ctx", [(i, i ^ bit ^ 1) for i in range(members)])
         if len(strands) < 2:
+            near_rows = ids.shape[0]
             strands.append(local(len(strands), *([] if bit == 4 else [ids])))
         ids = jnp.where(position & bit == 0, jnp.concatenate([ids, got]), jnp.concatenate([got, ids]))
         bit *= 2
-    while len(strands) < 2:
-        strands.append(local(len(strands)))
-    ids = jnp.where(position & 2 == 0, jnp.roll(ids, -1, axis=0), jnp.roll(ids, 1, axis=0))
-
-    (yg0, eg0, reads0), (yg1, eg1, reads1) = strands
+    (yg0, eg0, reads0), (yg1, eg1, reads1, near) = strands
     return pl.pallas_call(
-        functools.partial(finish_kernel, **sizes),
+        functools.partial(finish_kernel, near_rows=near_rows, **sizes),
         out_shape=jax.ShapeDtypeStruct((length, w_out.shape[1]), BF16),
-        in_specs=[vmem] * 12 + [hbm],
+        in_specs=[vmem] * 13 + [hbm],
         out_specs=vmem,
         scratch_shapes=[
             pltpu.SMEM(complement.shape, I32),
@@ -437,7 +504,7 @@
         compiler_params=params,
         name="finish",
     )(
-        *[held(a) for a in (ids, wide, xt, small, turn, w_out_v, reads0, yg0, eg0, reads1, yg1, eg1)],
+        *[held(a) for a in (ids, wide, xt, small, turn, w_out_v, reads0, yg0, eg0, reads1, yg1, eg1, near)],
         outside(complement),
     )
 

time: 22.8 us -> 22.5 us (0.987)
  the two profiles are of different devices: /device:TPU:0 before, /device:TPU:3 now
where the time goes in v4:
time: 22.5 us; the launch traced here: 22.2 us
  Pallas kernels  14.6 us (65%)
  starting transfers between devices  7.45 us (33%)
    pallas_call x1, Pallas kernels, on_device(): pl.pallas_call(functools.partial(finish_kernel, near_rows=near_rows, **si...  5.59 us
    ppermute x2, starting transfers between devices, on_device(): got = lax.ppermute(ids, 'ctx', [(i, i ^ bit ^ 1) for i in range(members)])  5.55 us
    pallas_call x2, Pallas kernels, local(): pl.pallas_call(functools.partial(local_kernel, strand=strand, **sizes), o...  5.3 us
    pallas_call x1, Pallas kernels, on_device(): pl.pallas_call(functools.partial(tables_kernel, **sizes), out_shape=[shap...  2.45 us
    ppermute x1, starting transfers between devices, on_device(): other = lax.ppermute(base_ids, 'ctx', across).reshape(1, length)  1.83 us
    pallas_call x1, Pallas kernels, on_device(): pl.pallas_call(codes_kernel, out_shape=[shape((inner + state, codes), BF1...  1.29 us
  transfers between devices with their start and end apart: 4, of which 0 were waited for; matrix products, arithmetic and copies ran while one was open for 0% of the time, Pallas kernels for 41%

profile of v4, /device:TPU:3, one launch (start us, length us, event | category | flops | bytes accessed | tf_op | source)
XLA Modules:
  0.0 22.2 jit_solution(9195882861531228372)
XLA Ops:
  0.0 1.8 %collective-permute-start = (s32[256]{0:T(256)}, s32[256]{0:T(256)S(1)}, u32[]{:S(2)}, u32[]{:S(2)}) collective-permute-start(s32[256]{0:T(256)} %base_ids_h.1), channel_id=1, source_target_pairs={{0,15},{1,2},{2,1},{3,4},{4,3},{5,6},{6,5},{7,8},{8,7},{9,10},{10,... | collective-permute-start | bytes 3080 | tf_op jit(solution)/shard_map/ppermute | solution.py:426
  1.8 2.5 %tables.1 = (s32[1,256]{1,0:T(1,128)S(1)}, bf16[2,64,2560]{2,1,0:T(8,128)(2,1)S(1)}, f32[40,1024]{1,0:T(8,128)S(1)}) custom-call(s32[256]{0:T(256)} %base_ids_h.1, s32[5]{0:T(128)} %comp_h.5, bf16[5,768]{1,0:T(8,128)(2,1)} %emb_h.1, bf16[768,768]{1,0:T(8,128)(2,1)} %w_gate_h.1, bf16[768,1024]{1,0:T(8,128)(2,1)} %w_mix_h.1, bf16[12,768]{1,0:T(8,128)(2,1)} %bitcast.2, ...), custom_call_target="tpu_custom_call" | custom-call | tf_op jit(solution)/shard_map/tables/pallas_call | solution.py:432
  4.3 0.0 collective-permute-done
  4.3 0.1 collective-permute-start.1
  4.4 1.3 %codes.1 = (bf16[896,640]{1,0:T(8,128)(2,1)S(1)}, bf16[128,128]{1,0:T(8,128)(2,1)S(1)}, bf16[768,768]{1,0:T(8,128)(2,1)S(1)}) custom-call(bf16[2,64,2560]{2,1,0:T(8,128)(2,1)S(1)} %get-tuple-element.19.wide, s32[2,256]{1,0:T(2,128)S(1)} %add_select_fusion.3._, s32[5]{0:T(128)} %comp_h.5, bf16[768,768]{1,0:T(8,128)(2,1)} %w_out_h.1), custom_call_target="tpu_custom_call" | custom-call | flops 2000000000 | tf_op jit(solution)/shard_map/codes/pallas_call | solution.py:454
  5.7 0.0 collective-permute-done.1
  5.7 1.7 %collective-permute-start.2 = (s32[4,256]{1,0:T(4,128)S(1)}, s32[4,256]{1,0:T(4,128)S(1)}, u32[]{:S(2)}, u32[]{:S(2)}) collective-permute-start(s32[4,256]{1,0:T(4,128)S(1)} %add_select_fusion.2.window), channel_id=1, source_target_pairs={{0,5},{1,4},{2,7},{3,6},{4,1},{5,0},{6,3},{7,2},{8,13},{9,12},{10,... | collective-permute-start | bytes 12296 | tf_op jit(solution)/shard_map/ppermute | solution.py:487
  7.5 2.3 %local.2 = (f32[2,256,768]{2,1,0:T(8,128)S(1)}, bf16[2,256,768]{2,1,0:T(8,128)(2,1)S(1)}, bf16[2,256,128]{2,1,0:T(8,128)(2,1)S(1)}) custom-call(s32[4,256]{1,0:T(4,128)S(1)} %add_select_fusion.2.window, bf16[2,64,2560]{2,1,0:T(8,128)(2,1)S(1)} %get-tuple-element.19.wide, f32[40,1024]{1,0:T(8,128)S(1)} %get-tuple-element.21.small), custom_call_target="tpu_custom_call" | custom-call | flops 4000000000 | tf_op jit(solution)/shard_map/local/pallas_call | solution.py:468
  9.8 0.0 collective-permute-done.2
  9.8 3.8 %collective-permute-start.3 = (s32[8,256]{1,0:T(8,128)S(1)}, s32[8,256]{1,0:T(8,128)S(1)}, u32[]{:S(2)}, u32[]{:S(2)}) collective-permute-start(s32[8,256]{1,0:T(8,128)S(1)} %add_select_fusion.1.rest_0_), channel_id=1, source_target_pairs={{0,9},{1,8},{2,11},{3,10},{4,13},{5,12},{6,15},{7,14},{8,1},{9,0},... | collective-permute-start | bytes 24584 | tf_op jit(solution)/shard_map/ppermute | solution.py:487
  13.6 3.0 %local.3 = (f32[2,256,768]{2,1,0:T(8,128)S(1)}, bf16[2,256,768]{2,1,0:T(8,128)(2,1)S(1)}, bf16[2,256,128]{2,1,0:T(8,128)(2,1)S(1)}, f32[120,256]{1,0:T(8,128)S(1)}) custom-call(s32[4,256]{1,0:T(4,128)S(1)} %add_select_fusion.2.window, bf16[2,64,2560]{2,1,0:T(8,128)(2,1)S(1)} %get-tuple-element.19.wide, f32[40,1024]{1,0:T(8,128)S(1)} %get-tuple-element.21.small, ...), custom_call_target="tpu_custom_call" | custom-call | flops 4000000000 | tf_op jit(solution)/shard_map/local/pallas_call | solution.py:468
  16.6 0.0 collective-permute-done.3
  16.6 5.6 %finish.1 = bf16[256,768]{1,0:T(8,128)(2,1)} custom-call(s32[16,256]{1,0:T(8,128)S(1)} %add_select_fusion.ids, bf16[2,64,2560]{2,1,0:T(8,128)(2,1)S(1)} %get-tuple-element.19.wide, bf16[896,640]{1,0:T(8,128)(2,1)S(1)} %get-tuple-element.20.xt, f32[40,1024]{1,0:T(8,128)S(1)} %get-tuple-element.21.small, bf16[128,128]{1,0:T(8,128)(2,1)S(1)} %get-tuple-element.22.turn, ...), custom_call_target="tpu_custom_call" | custom-call | tf_op jit(solution)/shard_map/finish/pallas_call | solution.py:494
  (4 shorter events, 0.0 us)
Async XLA Ops:
  0.0 4.3 %collective-permute-start = (s32[256]{0:T(256)}, s32[256]{0:T(256)S(1)}, u32[]{:S(2)}, u32[]{:S(2)}) collective-permute-start(s32[256]{0:T(256)} %base_ids_h.1), channel_id=1, source_target_pairs={{0,15},{1,2},{2,1},{3,4},{4,3},{5,6},{6,5},{7,8},{8,7},{9,10},{10,... | collective-permute-start | bytes 3080 | tf_op jit(solution)/shard_map/ppermute | solution.py:426
  4.3 1.4 %collective-permute-start.1 = (s32[2,256]{1,0:T(2,128)S(1)}, s32[2,256]{1,0:T(2,128)S(1)}, u32[]{:S(2)}, u32[]{:S(2)}) collective-permute-start(s32[2,256]{1,0:T(2,128)S(1)} %add_select_fusion.3._), channel_id=1, source_target_pairs={{0,1},{1,0},{2,3},{3,2},{4,5},{5,4},{6,7},{7,6},{8,9},{9,8},{10,11... | collective-permute-start | bytes 6152 | tf_op jit(solution)/shard_map/ppermute | solution.py:453
  5.7 4.0 %collective-permute-start.2 = (s32[4,256]{1,0:T(4,128)S(1)}, s32[4,256]{1,0:T(4,128)S(1)}, u32[]{:S(2)}, u32[]{:S(2)}) collective-permute-start(s32[4,256]{1,0:T(4,128)S(1)} %add_select_fusion.2.window), channel_id=1, source_target_pairs={{0,5},{1,4},{2,7},{3,6},{4,1},{5,0},{6,3},{7,2},{8,13},{9,12},{10,... | collective-permute-start | bytes 12296 | tf_op jit(solution)/shard_map/ppermute | solution.py:487
  9.8 6.8 %collective-permute-start.3 = (s32[8,256]{1,0:T(8,128)S(1)}, s32[8,256]{1,0:T(8,128)S(1)}, u32[]{:S(2)}, u32[]{:S(2)}) collective-permute-start(s32[8,256]{1,0:T(8,128)S(1)} %add_select_fusion.1.rest_0_), channel_id=1, source_target_pairs={{0,9},{1,8},{2,11},{3,10},{4,13},{5,12},{6,15},{7,14},{8,1},{9,0},... | collective-permute-start | bytes 24584 | tf_op jit(solution)/shard_map/ppermute | solution.py:487

commit v5 on v4

--- a/solution.py
+++ b/solution.py
@@ -312,7 +312,7 @@
 def finish_kernel(
     ids, wide, xt, small, turn, w_out, reads0, yg0, eg0, reads1, yg1, eg1, near, comp_h,
     out,
-    comp, moved, sem,
+    comp, moved, full, sem,
     *, heads, head_dim, state, near_rows,
 ):
     members, length = ids.shape
@@ -356,8 +356,13 @@
     edge_hot = jnp.concatenate([onehot_rows(d) for d in digits] * 2, axis=0)
     edge_hot = jnp.where((edge_lane < 3) | (edge_lane >= 125), edge_hot, 0.0)
     edge_hot = jnp.concatenate([edge_hot, pltpu.roll(edge_hot, 8, 1)], axis=0).astype(BF16)
-    edge = silu(dot(wide[:, :, : inner + state].reshape(128, inner + state), edge_hot, TN)).astype(BF16)
-    keys = jnp.concatenate([xt[inner:, :], edge[inner:]], axis=1)
+    edge = silu(dot(wide[:, :, : inner + state].reshape(128, inner + state), edge_hot, TN))
+    for tile, shift in enumerate((0, 125, 120, 117)):
+        at = slice(tile * 128, (tile + 1) * 128)
+        placed = (pltpu.roll(edge, shift, 1) if shift else edge).astype(BF16)
+        full[:, at] = jnp.where(iota((1, 128), 1) >= 125, placed, xt[:, at])
+    full[:, 512:] = xt[:, 512:]
+    keys = full[inner:, :]
     st = small[: 2 * heads, STEP_AT : STEP_AT + LETTER_ROWS]
     stepk = small[: 2 * heads, : letters * 128]
     ends = []
@@ -374,22 +379,24 @@
     first_strand = iota((span, 1), 0) < heads
     both = jnp.concatenate([sums[:, :128], sums[:, 128:]], axis=0)
     turned = dot(both.astype(BF16), turn[...])
-    for way, rim in enumerate((edge_ahead, edge_behind)):
+    for way, rim in enumerate((pltpu.roll(edge_ahead, 125, 1), edge_behind)):
         base = way * letters * span
         by_code = jnp.concatenate([both[base + v * span : base + (v + 1) * span] for v in range(letters)], axis=1)
         for v in range(letters):
             at = pl.multiple_of(comp[v] * 128, 128)
             moved[way, :, pl.ds(at, 128)] = turned[base + v * span : base + (v + 1) * span]
         by_code = jnp.where(first_strand, by_code, moved[way]) * stepk
-        rim = jnp.where(first_strand, rim, pltpu.roll(rim, 8, 1))
-        weights.append(jnp.concatenate([by_code, rim], axis=1).astype(BF16))
+        none = jnp.zeros_like(rim)
+        rims = [none] * letters
+        rims[1 - way] = jnp.where(first_strand, rim, 0.0)
+        rims[3 - way] = jnp.where(first_strand, 0.0, rim)
+        weights.append((by_code + jnp.concatenate(rims, axis=1)).astype(BF16))
     for strand in range(2):
         for way in range(2):
             scaled = []
             for head in range(heads):
                 at = slice(head * head_dim, (head + 1) * head_dim)
-                x_head = jnp.concatenate([xt[at, :], edge[at]], axis=1)
-                scaled.append(x_head * weights[way][strand * heads + head : strand * heads + head + 1, :])
+                scaled.append(full[at, :] * weights[way][strand * heads + head : strand * heads + head + 1, :])
             entering = dot(keys, jnp.concatenate(scaled, axis=0), NT).astype(BF16)
             reads, yg, eg = ((reads0, yg0, eg0), (reads1, yg1, eg1))[strand]
             carried = dot(reads[way], entering)
@@ -499,6 +506,7 @@
         scratch_shapes=[
             pltpu.SMEM(complement.shape, I32),
             VMEM((2, 2 * heads, codes), F32),
+            VMEM((inner + state, codes), BF16),
             pltpu.SemaphoreType.DMA(()),
         ],
         compiler_params=params,

time: 22.5 us -> 22 us (0.978)
  Pallas kernels: 14.6 us -> 14.2 us
    pallas_call x1, Pallas kernels: 5.59 us -> 5.11 us  [on_device(): pl.pallas_call(functools.partial(finish_kernel, near_rows=near_rows, **si...]
  transfers between devices with their start and end apart: 4 -> 4, of which waited for: 0 -> 0; matrix products, arithmetic and copies ran while one was open for 0% -> 0% of each run, Pallas kernels for 41% -> 42%
where the time goes in v5:
time: 22 us; the launch traced here: 21.8 us
  Pallas kernels  14.2 us (65%)
  starting transfers between devices  7.45 us (34%)
    ppermute x2, starting transfers between devices, on_device(): got = lax.ppermute(ids, 'ctx', [(i, i ^ bit ^ 1) for i in range(members)])  5.55 us
    pallas_call x2, Pallas kernels, local(): pl.pallas_call(functools.partial(local_kernel, strand=strand, **sizes), o...  5.3 us
    pallas_call x1, Pallas kernels, on_device(): pl.pallas_call(functools.partial(finish_kernel, near_rows=near_rows, **si...  5.11 us
    pallas_call x1, Pallas kernels, on_device(): pl.pallas_call(functools.partial(tables_kernel, **sizes), out_shape=[shap...  2.45 us
    ppermute x1, starting transfers between devices, on_device(): other = lax.ppermute(base_ids, 'ctx', across).reshape(1, length)  1.83 us
    pallas_call x1, Pallas kernels, on_device(): pl.pallas_call(codes_kernel, out_shape=[shape((inner + state, codes), BF1...  1.29 us
  transfers between devices with their start and end apart: 4, of which 0 were waited for; matrix products, arithmetic and copies ran while one was open for 0% of the time, Pallas kernels for 42%

profile of v5, /device:TPU:3, one launch (start us, length us, event | category | flops | bytes accessed | tf_op | source)
XLA Modules:
  0.0 21.8 jit_solution(17845543251610777192)
XLA Ops:
  0.0 1.8 %collective-permute-start = (s32[256]{0:T(256)}, s32[256]{0:T(256)S(1)}, u32[]{:S(2)}, u32[]{:S(2)}) collective-permute-start(s32[256]{0:T(256)} %base_ids_h.1), channel_id=1, source_target_pairs={{0,15},{1,2},{2,1},{3,4},{4,3},{5,6},{6,5},{7,8},{8,7},{9,10},{10,... | collective-permute-start | bytes 3080 | tf_op jit(solution)/shard_map/ppermute | solution.py:433
  1.8 2.5 %tables.1 = (s32[1,256]{1,0:T(1,128)S(1)}, bf16[2,64,2560]{2,1,0:T(8,128)(2,1)S(1)}, f32[40,1024]{1,0:T(8,128)S(1)}) custom-call(s32[256]{0:T(256)} %base_ids_h.1, s32[5]{0:T(128)} %comp_h.5, bf16[5,768]{1,0:T(8,128)(2,1)} %emb_h.1, bf16[768,768]{1,0:T(8,128)(2,1)} %w_gate_h.1, bf16[768,1024]{1,0:T(8,128)(2,1)} %w_mix_h.1, bf16[12,768]{1,0:T(8,128)(2,1)} %bitcast.2, ...), custom_call_target="tpu_custom_call" | custom-call | tf_op jit(solution)/shard_map/tables/pallas_call | solution.py:439
  4.3 0.0 collective-permute-done
  4.3 0.1 collective-permute-start.1
  4.4 1.3 %codes.1 = (bf16[896,640]{1,0:T(8,128)(2,1)S(1)}, bf16[128,128]{1,0:T(8,128)(2,1)S(1)}, bf16[768,768]{1,0:T(8,128)(2,1)S(1)}) custom-call(bf16[2,64,2560]{2,1,0:T(8,128)(2,1)S(1)} %get-tuple-element.19.wide, s32[2,256]{1,0:T(2,128)S(1)} %add_select_fusion.3._, s32[5]{0:T(128)} %comp_h.5, bf16[768,768]{1,0:T(8,128)(2,1)} %w_out_h.1), custom_call_target="tpu_custom_call" | custom-call | flops 2000000000 | tf_op jit(solution)/shard_map/codes/pallas_call | solution.py:461
  5.7 0.0 collective-permute-done.1
  5.7 1.7 %collective-permute-start.2 = (s32[4,256]{1,0:T(4,128)S(1)}, s32[4,256]{1,0:T(4,128)S(1)}, u32[]{:S(2)}, u32[]{:S(2)}) collective-permute-start(s32[4,256]{1,0:T(4,128)S(1)} %add_select_fusion.2.window), channel_id=1, source_target_pairs={{0,5},{1,4},{2,7},{3,6},{4,1},{5,0},{6,3},{7,2},{8,13},{9,12},{10,... | collective-permute-start | bytes 12296 | tf_op jit(solution)/shard_map/ppermute | solution.py:494
  7.5 2.3 %local.2 = (f32[2,256,768]{2,1,0:T(8,128)S(1)}, bf16[2,256,768]{2,1,0:T(8,128)(2,1)S(1)}, bf16[2,256,128]{2,1,0:T(8,128)(2,1)S(1)}) custom-call(s32[4,256]{1,0:T(4,128)S(1)} %add_select_fusion.2.window, bf16[2,64,2560]{2,1,0:T(8,128)(2,1)S(1)} %get-tuple-element.19.wide, f32[40,1024]{1,0:T(8,128)S(1)} %get-tuple-element.21.small), custom_call_target="tpu_custom_call" | custom-call | flops 4000000000 | tf_op jit(solution)/shard_map/local/pallas_call | solution.py:475
  9.8 0.0 collective-permute-done.2
  9.8 3.8 %collective-permute-start.3 = (s32[8,256]{1,0:T(8,128)S(1)}, s32[8,256]{1,0:T(8,128)S(1)}, u32[]{:S(2)}, u32[]{:S(2)}) collective-permute-start(s32[8,256]{1,0:T(8,128)S(1)} %add_select_fusion.1.rest_0_), channel_id=1, source_target_pairs={{0,9},{1,8},{2,11},{3,10},{4,13},{5,12},{6,15},{7,14},{8,1},{9,0},... | collective-permute-start | bytes 24584 | tf_op jit(solution)/shard_map/ppermute | solution.py:494
  13.6 3.0 %local.3 = (f32[2,256,768]{2,1,0:T(8,128)S(1)}, bf16[2,256,768]{2,1,0:T(8,128)(2,1)S(1)}, bf16[2,256,128]{2,1,0:T(8,128)(2,1)S(1)}, f32[120,256]{1,0:T(8,128)S(1)}) custom-call(s32[4,256]{1,0:T(4,128)S(1)} %add_select_fusion.2.window, bf16[2,64,2560]{2,1,0:T(8,128)(2,1)S(1)} %get-tuple-element.19.wide, f32[40,1024]{1,0:T(8,128)S(1)} %get-tuple-element.21.small, ...), custom_call_target="tpu_custom_call" | custom-call | flops 4000000000 | tf_op jit(solution)/shard_map/local/pallas_call | solution.py:475
  16.6 0.0 collective-permute-done.3
  16.6 5.1 %finish.1 = bf16[256,768]{1,0:T(8,128)(2,1)} custom-call(s32[16,256]{1,0:T(8,128)S(1)} %add_select_fusion.ids, bf16[2,64,2560]{2,1,0:T(8,128)(2,1)S(1)} %get-tuple-element.19.wide, bf16[896,640]{1,0:T(8,128)(2,1)S(1)} %get-tuple-element.20.xt, f32[40,1024]{1,0:T(8,128)S(1)} %get-tuple-element.21.small, bf16[128,128]{1,0:T(8,128)(2,1)S(1)} %get-tuple-element.22.turn, ...), custom_call_target="tpu_custom_call" | custom-call | tf_op jit(solution)/shard_map/finish/pallas_call | solution.py:501
  (4 shorter events, 0.0 us)
Async XLA Ops:
  0.0 4.3 %collective-permute-start = (s32[256]{0:T(256)}, s32[256]{0:T(256)S(1)}, u32[]{:S(2)}, u32[]{:S(2)}) collective-permute-start(s32[256]{0:T(256)} %base_ids_h.1), channel_id=1, source_target_pairs={{0,15},{1,2},{2,1},{3,4},{4,3},{5,6},{6,5},{7,8},{8,7},{9,10},{10,... | collective-permute-start | bytes 3080 | tf_op jit(solution)/shard_map/ppermute | solution.py:433
  4.3 1.4 %collective-permute-start.1 = (s32[2,256]{1,0:T(2,128)S(1)}, s32[2,256]{1,0:T(2,128)S(1)}, u32[]{:S(2)}, u32[]{:S(2)}) collective-permute-start(s32[2,256]{1,0:T(2,128)S(1)} %add_select_fusion.3._), channel_id=1, source_target_pairs={{0,1},{1,0},{2,3},{3,2},{4,5},{5,4},{6,7},{7,6},{8,9},{9,8},{10,11... | collective-permute-start | bytes 6152 | tf_op jit(solution)/shard_map/ppermute | solution.py:460
  5.7 4.0 %collective-permute-start.2 = (s32[4,256]{1,0:T(4,128)S(1)}, s32[4,256]{1,0:T(4,128)S(1)}, u32[]{:S(2)}, u32[]{:S(2)}) collective-permute-start(s32[4,256]{1,0:T(4,128)S(1)} %add_select_fusion.2.window), channel_id=1, source_target_pairs={{0,5},{1,4},{2,7},{3,6},{4,1},{5,0},{6,3},{7,2},{8,13},{9,12},{10,... | collective-permute-start | bytes 12296 | tf_op jit(solution)/shard_map/ppermute | solution.py:494
  9.8 6.8 %collective-permute-start.3 = (s32[8,256]{1,0:T(8,128)S(1)}, s32[8,256]{1,0:T(8,128)S(1)}, u32[]{:S(2)}, u32[]{:S(2)}) collective-permute-start(s32[8,256]{1,0:T(8,128)S(1)} %add_select_fusion.1.rest_0_), channel_id=1, source_target_pairs={{0,9},{1,8},{2,11},{3,10},{4,13},{5,12},{6,15},{7,14},{8,1},{9,0},... | collective-permute-start | bytes 24584 | tf_op jit(solution)/shard_map/ppermute | solution.py:494

commit v6 on v5

--- a/solution.py
+++ b/solution.py
@@ -69,11 +69,14 @@
     e16, ids_v, comp, emb, w_gate, w_mix, w_step, step_bias, rate, conv_w, conv_b, skip, gain_v, sems,
     *, heads, head_dim, state,
 ):
+    half = emb.shape[1] // 2
+    first, rest = pl.ds(0, half), pl.ds(half, half)
     pairs = [
-        (emb_h, emb), (comp_h, comp), (w_mix_h, w_mix), (w_step_h, w_step), (step_bias_h, step_bias), (rate_h, rate),
+        (emb_h, emb), (comp_h, comp), (w_mix_h.at[first], w_mix.at[first]), (w_step_h, w_step), (step_bias_h, step_bias), (rate_h, rate),
         (skip_h, skip), (conv_w_h, conv_w), (conv_b_h, conv_b), (w_gate_h, w_gate), (base_ids_h, ids_v),
         (norm_gain_h, gain_v),
     ]
+    pairs.insert(3, (w_mix_h.at[rest], w_mix.at[rest]))
     copies = [pltpu.make_async_copy(a, b, sems.at[n]) for n, (a, b) in enumerate(pairs)]
     for copy in copies:
         copy.start()
@@ -85,9 +88,11 @@
     for v in range(letters):
         e16[LETTER_ROWS + v : LETTER_ROWS + v + 1, :] = e16[pl.ds(comp[v], 1), :]
     rows = e16[...].astype(BF16)
-    for copy in copies[2:9]:
+    copies[2].wait()
+    mix = dot(rows[:, :half], w_mix[first, :])
+    for copy in copies[3:10]:
         copy.wait()
-    mix = dot(rows, w_mix[...]).astype(BF16).astype(F32)
+    mix = (mix + dot(rows[:, half:], w_mix[rest, :])).astype(BF16).astype(F32)
     raw = dot(rows, w_step[...], NT) + step_bias[...].reshape(1, heads)
     step = jnp.maximum(raw, 0.0) + jnp.log1p(jnp.exp(-jnp.abs(raw)))
     decay_t = jnp.transpose(-step * rate[...].reshape(1, heads))
@@ -113,15 +118,15 @@
         high, low = split(jnp.concatenate(weighted, axis=0))
         both = jnp.concatenate([high, low], axis=0)
         wide[strand, :, :width] = both.astype(BF16)
-    copies[9].wait()
+    copies[10].wait()
     gate = silu(dot(rows, w_gate[...]).astype(BF16).astype(F32))
     gates = split(gate)
     for strand in range(2):
         at = slice(strand * LETTER_ROWS, (strand + 1) * LETTER_ROWS)
-        rest = jnp.zeros((3 * LETTER_ROWS, 2 * inner), F32)
+        blank = jnp.zeros((3 * LETTER_ROWS, 2 * inner), F32)
         parts = [jnp.concatenate([gates[n][at], steps[n][at]], axis=1) for n in range(2)]
-        wide[strand, :, width:] = jnp.concatenate([rest, parts[0], rest, parts[1]], axis=0).astype(BF16)
-    for copy in copies[10:]:
+        wide[strand, :, width:] = jnp.concatenate([blank, parts[0], blank, parts[1]], axis=0).astype(BF16)
+    for copy in copies[11:]:
         copy.wait()
     own[...] = ids_v[...].reshape(own.shape)
     small[GAIN_AT : GAIN_AT + 1, :inner] = gain_v[...].reshape(1, inner)
@@ -451,7 +456,7 @@
             pltpu.SMEM(complement.shape, I32),
         ]
         + [VMEM(a.shape, a.dtype) for a in given[2:12]]
-        + [pltpu.SemaphoreType.DMA((len(given),))],
+        + [pltpu.SemaphoreType.DMA((len(given) + 1,))],
         compiler_params=params,
         name="tables",
     )(*[outside(a) for a in given])

time: 22 us -> 22 us (level)
  transfers between devices with their start and end apart: 4 -> 4, of which waited for: 0 -> 0; matrix products, arithmetic and copies ran while one was open for 0% -> 0% of each run, Pallas kernels for 42% -> 41%
where the time goes in v6:
time: 22 us; the launch traced here: 21.8 us
  Pallas kernels  14 us (64%)
  starting transfers between devices  7.57 us (34%)
    ppermute x2, starting transfers between devices, on_device(): got = lax.ppermute(ids, 'ctx', [(i, i ^ bit ^ 1) for i in range(members)])  5.67 us
    pallas_call x2, Pallas kernels, local(): pl.pallas_call(functools.partial(local_kernel, strand=strand, **sizes), o...  5.31 us
    pallas_call x1, Pallas kernels, on_device(): pl.pallas_call(functools.partial(finish_kernel, near_rows=near_rows, **si...  5.11 us
    pallas_call x1, Pallas kernels, on_device(): pl.pallas_call(functools.partial(tables_kernel, **sizes), out_shape=[shap...  2.33 us
    ppermute x1, starting transfers between devices, on_device(): other = lax.ppermute(base_ids, 'ctx', across).reshape(1, length)  1.83 us
    pallas_call x1, Pallas kernels, on_device(): pl.pallas_call(codes_kernel, out_shape=[shape((inner + state, codes), BF1...  1.29 us
  transfers between devices with their start and end apart: 4, of which 0 were waited for; matrix products, arithmetic and copies ran while one was open for 0% of the time, Pallas kernels for 41%

profile of v6, /device:TPU:3, one launch (start us, length us, event | category | flops | bytes accessed | tf_op | source)
XLA Modules:
  0.0 21.8 jit_solution(15204114697769996587)
XLA Ops:
  0.0 1.8 %collective-permute-start = (s32[256]{0:T(256)}, s32[256]{0:T(256)S(1)}, u32[]{:S(2)}, u32[]{:S(2)}) collective-permute-start(s32[256]{0:T(256)} %base_ids_h.1), channel_id=1, source_target_pairs={{0,15},{1,2},{2,1},{3,4},{4,3},{5,6},{6,5},{7,8},{8,7},{9,10},{10,... | collective-permute-start | bytes 3080 | tf_op jit(solution)/shard_map/ppermute | solution.py:438
  1.8 2.3 %tables.1 = (s32[1,256]{1,0:T(1,128)S(1)}, bf16[2,64,2560]{2,1,0:T(8,128)(2,1)S(1)}, f32[40,1024]{1,0:T(8,128)S(1)}) custom-call(s32[256]{0:T(256)} %base_ids_h.1, s32[5]{0:T(128)} %comp_h.5, bf16[5,768]{1,0:T(8,128)(2,1)} %emb_h.1, bf16[768,768]{1,0:T(8,128)(2,1)} %w_gate_h.1, bf16[768,1024]{1,0:T(8,128)(2,1)} %w_mix_h.1, bf16[12,768]{1,0:T(8,128)(2,1)} %bitcast.2, ...), custom_call_target="tpu_custom_call" | custom-call | tf_op jit(solution)/shard_map/tables/pallas_call | solution.py:444
  4.2 0.0 collective-permute-done
  4.2 0.1 collective-permute-start.1
  4.3 1.3 %codes.1 = (bf16[896,640]{1,0:T(8,128)(2,1)S(1)}, bf16[128,128]{1,0:T(8,128)(2,1)S(1)}, bf16[768,768]{1,0:T(8,128)(2,1)S(1)}) custom-call(bf16[2,64,2560]{2,1,0:T(8,128)(2,1)S(1)} %get-tuple-element.19.wide, s32[2,256]{1,0:T(2,128)S(1)} %add_select_fusion.3._, s32[5]{0:T(128)} %comp_h.5, bf16[768,768]{1,0:T(8,128)(2,1)} %w_out_h.1), custom_call_target="tpu_custom_call" | custom-call | flops 2000000000 | tf_op jit(solution)/shard_map/codes/pallas_call | solution.py:466
  5.6 0.0 collective-permute-done.1
  5.6 1.7 %collective-permute-start.2 = (s32[4,256]{1,0:T(4,128)S(1)}, s32[4,256]{1,0:T(4,128)S(1)}, u32[]{:S(2)}, u32[]{:S(2)}) collective-permute-start(s32[4,256]{1,0:T(4,128)S(1)} %add_select_fusion.2.window), channel_id=1, source_target_pairs={{0,5},{1,4},{2,7},{3,6},{4,1},{5,0},{6,3},{7,2},{8,13},{9,12},{10,... | collective-permute-start | bytes 12296 | tf_op jit(solution)/shard_map/ppermute | solution.py:499
  7.3 2.3 %local.2 = (f32[2,256,768]{2,1,0:T(8,128)S(1)}, bf16[2,256,768]{2,1,0:T(8,128)(2,1)S(1)}, bf16[2,256,128]{2,1,0:T(8,128)(2,1)S(1)}) custom-call(s32[4,256]{1,0:T(4,128)S(1)} %add_select_fusion.2.window, bf16[2,64,2560]{2,1,0:T(8,128)(2,1)S(1)} %get-tuple-element.19.wide, f32[40,1024]{1,0:T(8,128)S(1)} %get-tuple-element.21.small), custom_call_target="tpu_custom_call" | custom-call | flops 4000000000 | tf_op jit(solution)/shard_map/local/pallas_call | solution.py:480
  9.6 0.0 collective-permute-done.2
  9.7 3.9 %collective-permute-start.3 = (s32[8,256]{1,0:T(8,128)S(1)}, s32[8,256]{1,0:T(8,128)S(1)}, u32[]{:S(2)}, u32[]{:S(2)}) collective-permute-start(s32[8,256]{1,0:T(8,128)S(1)} %add_select_fusion.1.rest_0_), channel_id=1, source_target_pairs={{0,9},{1,8},{2,11},{3,10},{4,13},{5,12},{6,15},{7,14},{8,1},{9,0},... | collective-permute-start | bytes 24584 | tf_op jit(solution)/shard_map/ppermute | solution.py:499
  13.6 3.0 %local.3 = (f32[2,256,768]{2,1,0:T(8,128)S(1)}, bf16[2,256,768]{2,1,0:T(8,128)(2,1)S(1)}, bf16[2,256,128]{2,1,0:T(8,128)(2,1)S(1)}, f32[120,256]{1,0:T(8,128)S(1)}) custom-call(s32[4,256]{1,0:T(4,128)S(1)} %add_select_fusion.2.window, bf16[2,64,2560]{2,1,0:T(8,128)(2,1)S(1)} %get-tuple-element.19.wide, f32[40,1024]{1,0:T(8,128)S(1)} %get-tuple-element.21.small, ...), custom_call_target="tpu_custom_call" | custom-call | flops 4000000000 | tf_op jit(solution)/shard_map/local/pallas_call | solution.py:480
  16.6 0.0 collective-permute-done.3
  16.6 5.1 %finish.1 = bf16[256,768]{1,0:T(8,128)(2,1)} custom-call(s32[16,256]{1,0:T(8,128)S(1)} %add_select_fusion.ids, bf16[2,64,2560]{2,1,0:T(8,128)(2,1)S(1)} %get-tuple-element.19.wide, bf16[896,640]{1,0:T(8,128)(2,1)S(1)} %get-tuple-element.20.xt, f32[40,1024]{1,0:T(8,128)S(1)} %get-tuple-element.21.small, bf16[128,128]{1,0:T(8,128)(2,1)S(1)} %get-tuple-element.22.turn, ...), custom_call_target="tpu_custom_call" | custom-call | tf_op jit(solution)/shard_map/finish/pallas_call | solution.py:506
  (4 shorter events, 0.0 us)
Async XLA Ops:
  0.0 4.2 %collective-permute-start = (s32[256]{0:T(256)}, s32[256]{0:T(256)S(1)}, u32[]{:S(2)}, u32[]{:S(2)}) collective-permute-start(s32[256]{0:T(256)} %base_ids_h.1), channel_id=1, source_target_pairs={{0,15},{1,2},{2,1},{3,4},{4,3},{5,6},{6,5},{7,8},{8,7},{9,10},{10,... | collective-permute-start | bytes 3080 | tf_op jit(solution)/shard_map/ppermute | solution.py:438
  4.2 1.4 %collective-permute-start.1 = (s32[2,256]{1,0:T(2,128)S(1)}, s32[2,256]{1,0:T(2,128)S(1)}, u32[]{:S(2)}, u32[]{:S(2)}) collective-permute-start(s32[2,256]{1,0:T(2,128)S(1)} %add_select_fusion.3._), channel_id=1, source_target_pairs={{0,1},{1,0},{2,3},{3,2},{4,5},{5,4},{6,7},{7,6},{8,9},{9,8},{10,11... | collective-permute-start | bytes 6152 | tf_op jit(solution)/shard_map/ppermute | solution.py:465
  5.6 4.0 %collective-permute-start.2 = (s32[4,256]{1,0:T(4,128)S(1)}, s32[4,256]{1,0:T(4,128)S(1)}, u32[]{:S(2)}, u32[]{:S(2)}) collective-permute-start(s32[4,256]{1,0:T(4,128)S(1)} %add_select_fusion.2.window), channel_id=1, source_target_pairs={{0,5},{1,4},{2,7},{3,6},{4,1},{5,0},{6,3},{7,2},{8,13},{9,12},{10,... | collective-permute-start | bytes 12296 | tf_op jit(solution)/shard_map/ppermute | solution.py:499
  9.7 6.9 %collective-permute-start.3 = (s32[8,256]{1,0:T(8,128)S(1)}, s32[8,256]{1,0:T(8,128)S(1)}, u32[]{:S(2)}, u32[]{:S(2)}) collective-permute-start(s32[8,256]{1,0:T(8,128)S(1)} %add_select_fusion.1.rest_0_), channel_id=1, source_target_pairs={{0,9},{1,8},{2,11},{3,10},{4,13},{5,12},{6,15},{7,14},{8,1},{9,0},... | collective-permute-start | bytes 24584 | tf_op jit(solution)/shard_map/ppermute | solution.py:499
